TPU v7x, 32 devices: a whole 2x2x4 slice. The times are simulated.
32 devices in a mesh: tm: 4 (over y, x), map: 8 (over z, core).
Axes of the slice: x: 2, y: 2, z: 4, core: 2. Of those that a mesh axis runs over, the one named last changes fastest.
Arguments:
- tiles: float32 [4, 2, 64, 4, 128, 128], P('tm', None, 'map'), may hold values from -0.25 to 0.25
- columns: int32 [4, 2, 64, 4], P('tm', None, 'map'), may hold values from 0 to 63, as said below
- window_steps: int32 [4], P('tm'), may hold values from 1 to 2
- direction: float32 [8, 64, 128], P(None, 'map'), may hold values from -6 to 6
- forcing: float32 [4, 2, 64, 128], P('tm', None, 'map'), may hold values from 0.05 to 0.5
- observe: float32 [4, 2, 64, 128], P('tm', None, 'map'), may hold values from 0.1 to 1
Outputs:
- hessian_action: float32 [8, 64, 128], P('tm', 'map')
Inputs may be any that keep to these rules, and one draw needn't show every extreme that they name: `columns`: every column index of block row r lies between p * 8 - 2 and (p + 1) * 8 + 1, where p = r // 8.
All inputs are finite; a program needn't handle non-finite values.
Results may differ from a plain program's by a relative error of at most 0.0001.
Values sent between devices are 32-bit elements; how exact they have to be, the bound alone decides.
A program may use at most 64 MiB of HBM per device.

v0:
```python
import jax
import jax.numpy as jnp
from jax import lax
from jax.sharding import PartitionSpec as P

HALO = 2


def extended_2(block, sides, width):
    for axis, dim in sides:
        count = lax.axis_size(axis)
        forward = [(i, i + 1) for i in range(count - 1)]
        backward = [(target, source) for source, target in forward]
        low = lax.ppermute(
            lax.slice_in_dim(block, block.shape[dim] - width, None, axis=dim), axis, forward
        )
        high = lax.ppermute(lax.slice_in_dim(block, 0, width, axis=dim), axis, backward)
        block = jnp.concatenate([low, block, high], axis=dim)
    return block


def from_behind(value, axis, steps):
    count = lax.axis_size(axis)
    leading, last = (max(0, -steps), min(count, count - steps))
    return lax.ppermute(value, axis, [(source, source + steps) for source in range(leading, last)])


def shards(tiles, columns, window_steps, direction, forcing, observe):
    nblock = direction.shape[1]
    tile_size = direction.shape[2]
    step_count = tiles.shape[1]
    slots = tiles.shape[3]
    window_count = lax.axis_size("tm")
    partition = lax.axis_index("map")
    first_block = partition * nblock - HALO
    local_cols = columns[0] - first_block
    active_steps = window_steps[0]
    positions = jnp.arange(nblock + 2 * HALO, dtype=jnp.int32)
    selectors = (
        local_cols.reshape(step_count, nblock * slots)[:, :, None] == positions[None, None, :]
    ).astype(jnp.float32)
    incoming = jnp.zeros(direction.shape, jnp.float32)
    history = None
    for sweep_turn in range(window_count):
        current = incoming
        forward_states = [incoming]
        for forward_step_index in range(step_count):
            extended = extended_2(current, (("map", 1),), HALO)
            picked = jnp.take(extended, local_cols[forward_step_index].reshape(-1), axis=1)
            picked = picked.reshape(current.shape[0], nblock, slots, tile_size)
            product = jnp.einsum(
                "dbje,bjce->dbc",
                picked,
                tiles[0, forward_step_index],
                precision=lax.Precision.HIGHEST,
            )
            forward_updated = product + forcing[0, forward_step_index][None] * direction
            current = jnp.where(forward_step_index < active_steps, forward_updated, current)
            forward_states.append(current)
        history = jnp.stack(forward_states)
        if sweep_turn + 1 < window_count:
            incoming = from_behind(current, "tm", 1)
    incoming = jnp.zeros(direction.shape, jnp.float32)
    gradient = None
    for sweep_turn in range(window_count):
        carried = incoming
        backward_gradient = jnp.zeros(incoming.shape, jnp.float32)
        for step_index in range(step_count - 1, -1, -1):
            active = step_index < active_steps
            adjoint = carried + observe[0, step_index][None] * history[step_index + 1]
            backward_gradient = backward_gradient + jnp.where(
                active, forcing[0, step_index][None] * adjoint, 0.0
            )
            contrib = jnp.einsum(
                "dbc,bjce->dbje", adjoint, tiles[0, step_index], precision=lax.Precision.HIGHEST
            )
            contrib = contrib.reshape(incoming.shape[0], nblock * slots, tile_size)
            spread = jnp.einsum(
                "dre,rx->dxe", contrib, selectors[step_index], precision=lax.Precision.HIGHEST
            )
            rim_parts = jnp.concatenate([spread[:, :HALO], spread[:, nblock + HALO :]], axis=1)
            returned = extended_2(rim_parts, (("map", 1),), HALO)
            updated = spread[:, HALO : HALO + nblock]
            updated = updated + jnp.pad(returned[:, :HALO], ((0, 0), (0, nblock - HALO), (0, 0)))
            updated = updated + jnp.pad(
                returned[:, 3 * HALO :], ((0, 0), (nblock - HALO, 0), (0, 0))
            )
            carried = jnp.where(active, updated, carried)
        carried, gradient = (carried, backward_gradient)
        if sweep_turn + 1 < window_count:
            incoming = from_behind(carried, "tm", -1)
    return lax.psum_scatter(gradient, "tm", scatter_dimension=0, tiled=True)


def solution(mesh):
    placed = (
        P("tm", None, "map", None, None, None),
        P("tm", None, "map", None),
        P("tm"),
        P(None, "map", None),
        P("tm", None, "map", None),
        P("tm", None, "map", None),
    )
    return jax.shard_map(
        shards, mesh=mesh, in_specs=placed, out_specs=P("tm", "map", None), check_vma=False
    )
```

profile of v0, /device:TPU:1, one launch (start us, length us, event | category | flops | bytes accessed | tf_op | source)
XLA Modules:
  0.0 203.0 jit_solution(2243519488272465876)
XLA Ops:
  0.0 4.7 %collective-permute-start = (f32[8,2,128]{2,0,1:T(8,128)S(1)}, f32[8,2,128]{2,0,1:T(8,128)S(1)}, u32[]{:S(2)}, u32[]{:S(2)}) collective-permute-start(f32[8,2,128]{2,0,1:T(8,128)S(1)} %broadcast.45), channel_id=1, source_target_pairs={{0,1},{1,2},{2,3},{3,4},{4,5},{5,6},{6,7},{8,9},{9,10},{10,11},{11... | collective-permute-start | bytes 24584 | tf_op jit(solution)/shard_map/ppermute | solution.py:14
  4.7 1.9 collective-permute-start.1
  10.4 3.4 %fusion.117 = f32[8,8,128]{2,0,1:T(8,128)S(1)} fusion(f32[8,8,4,128]{3,0,2,1:T(8,128)S(1)} %bitcast.304, f32[1,2,8,4,128,128]{5,4,3,2,1,0:T(8,128)} %param.8, f32[8,8,128]{2,1,0:T(8,128)} %param.11, f32[8,128]{1,0:T(8,128)S(1)} %get-tuple-element.37, pred[]{:T(512)} %bitcast.2), kind=kOutput, calls=%fused_computation.77 | convolution fusion | flops 50356224 | bytes 2298368 | tf_op jit(solution)/shard_map/dbje,bjce->dbc/dot_general | solution.py:51
  13.8 3.1 %collective-permute-start.2 = (f32[8,2,128]{2,0,1:T(8,128)S(1)}, f32[8,2,128]{2,0,1:T(8,128)S(1)}, u32[]{:S(2)}, u32[]{:S(2)}) collective-permute-start(f32[8,2,128]{2,0,1:T(8,128)S(1)} %get-tuple-element.32), channel_id=1, source_target_pairs={{0,1},{1,2},{2,3},{3,4},{4,5},{5,6},{6,7},{8,9},{9,10},{10,11},{11... | collective-permute-start | bytes 24584 | tf_op jit(solution)/shard_map/ppermute | solution.py:14
  16.9 1.9 collective-permute-start.3
  18.9 3.0 %collective-permute-done.3 = f32[8,2,128]{2,0,1:T(8,128)S(1)} collective-permute-done((f32[8,2,128]{2,0,1:T(8,128)S(1)}, f32[8,2,128]{2,0,1:T(8,128)S(1)}, u32[]{:S(2)}, u32[]{:S(2)}) %collective-permute-start.3) | collective-permute-done | bytes 8224 | tf_op jit(solution)/shard_map/ppermute | solution.py:17
  22.6 3.4 %fusion.93 = f32[8,8,128]{2,0,1:T(8,128)S(1)} fusion(f32[8,8,128]{2,0,1:T(8,128)S(1)} %fusion.117, f32[8,8,4,128]{3,0,2,1:T(8,128)S(1)} %bitcast.297, f32[1,2,8,4,128,128]{5,4,3,2,1,0:T(8,128)} %param.8, f32[8,8,128]{2,1,0:T(8,128)} %param.11, f32[8,128]{1,0:T(8,128)S(1)} %get-tuple-element.36, pred[]{:T(512)} %bitcast), kind=kOutput, calls=%fused_computation.69 | convolution fusion | flops 50356224 | bytes 2331136 | tf_op jit(solution)/shard_map/dbje,bjce->dbc/dot_general | solution.py:51
  26.0 3.1 %collective-permute-start.4 = (f32[8,8,128]{2,0,1:T(8,128)S(1)}, f32[8,8,128]{2,0,1:T(8,128)S(1)}, u32[]{:S(2)}, u32[]{:S(2)}) collective-permute-start(f32[8,8,128]{2,0,1:T(8,128)S(1)} %fusion.93), channel_id=1, source_target_pairs={{0,8},{8,16},{16,24},{1,9},{9,17},{17,25},{2,10},{10,18},{18,26},{... | collective-permute-start | bytes 98312 | tf_op jit(solution)/shard_map/ppermute | solution.py:25
  30.1 2.8 %collective-permute-start.5 = (f32[8,2,128]{2,0,1:T(8,128)S(1)}, f32[8,2,128]{2,0,1:T(8,128)S(1)}, u32[]{:S(2)}, u32[]{:S(2)}) collective-permute-start(f32[8,2,128]{2,0,1:T(8,128)S(1)} %get-tuple-element.30), channel_id=1, source_target_pairs={{0,1},{1,2},{2,3},{3,4},{4,5},{5,6},{6,7},{8,9},{9,10},{10,11},{11... | collective-permute-start | bytes 24584 | tf_op jit(solution)/shard_map/ppermute | solution.py:14
  32.9 1.9 collective-permute-start.6
  34.8 3.0 %collective-permute-done.6 = f32[8,2,128]{2,0,1:T(8,128)S(1)} collective-permute-done((f32[8,2,128]{2,0,1:T(8,128)S(1)}, f32[8,2,128]{2,0,1:T(8,128)S(1)}, u32[]{:S(2)}, u32[]{:S(2)}) %collective-permute-start.6) | collective-permute-done | bytes 8224 | tf_op jit(solution)/shard_map/ppermute | solution.py:17
  38.6 3.4 %fusion.111 = f32[8,8,128]{2,0,1:T(8,128)S(1)} fusion(f32[8,8,128]{2,0,1:T(8,128)S(1)} %collective-permute-done.4, f32[8,8,4,128]{3,0,2,1:T(8,128)S(1)} %bitcast.300, f32[1,2,8,4,128,128]{5,4,3,2,1,0:T(8,128)} %param.8, f32[8,8,128]{2,1,0:T(8,128)S(1)} %copy-done.1, f32[8,128]{1,0:T(8,128)S(1)} %get-tuple-element.37, pred[]{:T(512)} %bitcast.2), kind=kOutput, calls=%fused_computation.75 | convolution fusion | flops 50356224 | bytes 2331136 | tf_op jit(solution)/shard_map/dbje,bjce->dbc/dot_general | solution.py:51
  42.0 1.9 collective-permute-start.7
  44.0 2.4 %collective-permute-start.8 = (f32[8,2,128]{2,0,1:T(8,128)S(1)}, f32[8,2,128]{2,0,1:T(8,128)S(1)}, u32[]{:S(2)}, u32[]{:S(2)}) collective-permute-start(f32[8,2,128]{2,0,1:T(8,128)S(1)} %get-tuple-element.29), channel_id=1, source_target_pairs={{1,0},{2,1},{3,2},{4,3},{5,4},{6,5},{7,6},{9,8},{10,9},{11,10},{12... | collective-permute-start | bytes 24584 | tf_op jit(solution)/shard_map/ppermute | solution.py:17
  46.3 2.6 %collective-permute-done.8 = f32[8,2,128]{2,0,1:T(8,128)S(1)} collective-permute-done((f32[8,2,128]{2,0,1:T(8,128)S(1)}, f32[8,2,128]{2,0,1:T(8,128)S(1)}, u32[]{:S(2)}, u32[]{:S(2)}) %collective-permute-start.8) | collective-permute-done | bytes 8224 | tf_op jit(solution)/shard_map/ppermute | solution.py:17
  49.6 3.4 %fusion.87 = f32[8,8,128]{2,0,1:T(8,128)S(1)} fusion(f32[8,8,128]{2,0,1:T(8,128)S(1)} %fusion.111, f32[8,8,4,128]{3,0,2,1:T(8,128)S(1)} %bitcast.301, f32[1,2,8,4,128,128]{5,4,3,2,1,0:T(8,128)} %param.8, f32[8,8,128]{2,1,0:T(8,128)S(1)} %copy-done.1, f32[8,128]{1,0:T(8,128)S(1)} %get-tuple-element.36, pred[]{:T(512)} %bitcast), kind=kOutput, calls=%fused_computation.67 | convolution fusion | flops 50356224 | bytes 2331136 | tf_op jit(solution)/shard_map/dbje,bjce->dbc/dot_general | solution.py:51
  53.0 3.9 %collective-permute-start.9 = (f32[8,8,128]{2,0,1:T(8,128)S(1)}, f32[8,8,128]{2,0,1:T(8,128)S(1)}, u32[]{:S(2)}, u32[]{:S(2)}) collective-permute-start(f32[8,8,128]{2,0,1:T(8,128)S(1)} %fusion.87), channel_id=1, source_target_pairs={{0,8},{8,16},{16,24},{1,9},{9,17},{17,25},{2,10},{10,18},{18,26},{... | collective-permute-start | bytes 98312 | tf_op jit(solution)/shard_map/ppermute | solution.py:25
  58.0 2.8 %collective-permute-start.10 = (f32[8,2,128]{2,0,1:T(8,128)S(1)}, f32[8,2,128]{2,0,1:T(8,128)S(1)}, u32[]{:S(2)}, u32[]{:S(2)}) collective-permute-start(f32[8,2,128]{2,0,1:T(8,128)S(1)} %get-tuple-element.26), channel_id=1, source_target_pairs={{0,1},{1,2},{2,3},{3,4},{4,5},{5,6},{6,7},{8,9},{9,10},{10,11},{11... | collective-permute-start | bytes 24584 | tf_op jit(solution)/shard_map/ppermute | solution.py:14
  60.8 1.9 collective-permute-start.11
  62.7 3.0 %collective-permute-done.11 = f32[8,2,128]{2,0,1:T(8,128)S(1)} collective-permute-done((f32[8,2,128]{2,0,1:T(8,128)S(1)}, f32[8,2,128]{2,0,1:T(8,128)S(1)}, u32[]{:S(2)}, u32[]{:S(2)}) %collective-permute-start.11) | collective-permute-done | bytes 8224 | tf_op jit(solution)/shard_map/ppermute | solution.py:17
  66.5 3.4 %fusion.105 = f32[8,8,128]{2,0,1:T(8,128)S(1)} fusion(f32[8,8,128]{2,0,1:T(8,128)S(1)} %collective-permute-done.9, f32[8,8,4,128]{3,0,2,1:T(8,128)S(1)} %bitcast.302, f32[1,2,8,4,128,128]{5,4,3,2,1,0:T(8,128)} %param.8, f32[8,8,128]{2,1,0:T(8,128)S(1)} %copy-done.1, f32[8,128]{1,0:T(8,128)S(1)} %get-tuple-element.37, pred[]{:T(512)} %bitcast.2), kind=kOutput, calls=%fused_computation.73 | convolution fusion | flops 50356224 | bytes 2331136 | tf_op jit(solution)/shard_map/dbje,bjce->dbc/dot_general | solution.py:51
  69.9 1.9 collective-permute-start.12
  71.8 2.4 %collective-permute-start.13 = (f32[8,2,128]{2,0,1:T(8,128)S(1)}, f32[8,2,128]{2,0,1:T(8,128)S(1)}, u32[]{:S(2)}, u32[]{:S(2)}) collective-permute-start(f32[8,2,128]{2,0,1:T(8,128)S(1)} %get-tuple-element.25), channel_id=1, source_target_pairs={{1,0},{2,1},{3,2},{4,3},{5,4},{6,5},{7,6},{9,8},{10,9},{11,10},{12... | collective-permute-start | bytes 24584 | tf_op jit(solution)/shard_map/ppermute | solution.py:17
  74.2 2.6 %collective-permute-done.13 = f32[8,2,128]{2,0,1:T(8,128)S(1)} collective-permute-done((f32[8,2,128]{2,0,1:T(8,128)S(1)}, f32[8,2,128]{2,0,1:T(8,128)S(1)}, u32[]{:S(2)}, u32[]{:S(2)}) %collective-permute-start.13) | collective-permute-done | bytes 8224 | tf_op jit(solution)/shard_map/ppermute | solution.py:17
  77.5 3.4 %fusion.81 = f32[8,8,128]{2,0,1:T(8,128)S(1)} fusion(f32[8,8,128]{2,0,1:T(8,128)S(1)} %fusion.105, f32[8,8,4,128]{3,0,2,1:T(8,128)S(1)} %bitcast.303, f32[1,2,8,4,128,128]{5,4,3,2,1,0:T(8,128)} %param.8, f32[8,8,128]{2,1,0:T(8,128)S(1)} %copy-done.1, f32[8,128]{1,0:T(8,128)S(1)} %get-tuple-element.36, pred[]{:T(512)} %bitcast), kind=kOutput, calls=%fused_computation.65 | convolution fusion | flops 50356224 | bytes 2331136 | tf_op jit(solution)/shard_map/dbje,bjce->dbc/dot_general | solution.py:51
  80.9 4.0 %collective-permute-start.14 = (f32[8,8,128]{2,0,1:T(8,128)S(1)}, f32[8,8,128]{2,0,1:T(8,128)S(1)}, u32[]{:S(2)}, u32[]{:S(2)}) collective-permute-start(f32[8,8,128]{2,0,1:T(8,128)S(1)} %fusion.81), channel_id=1, source_target_pairs={{0,8},{8,16},{16,24},{1,9},{9,17},{17,25},{2,10},{10,18},{18,26},{... | collective-permute-start | bytes 98312 | tf_op jit(solution)/shard_map/ppermute | solution.py:25
  85.9 2.8 %collective-permute-start.15 = (f32[8,2,128]{2,0,1:T(8,128)S(1)}, f32[8,2,128]{2,0,1:T(8,128)S(1)}, u32[]{:S(2)}, u32[]{:S(2)}) collective-permute-start(f32[8,2,128]{2,0,1:T(8,128)S(1)} %get-tuple-element.22), channel_id=1, source_target_pairs={{0,1},{1,2},{2,3},{3,4},{4,5},{5,6},{6,7},{8,9},{9,10},{10,11},{11... | collective-permute-start | bytes 24584 | tf_op jit(solution)/shard_map/ppermute | solution.py:14
  88.7 2.1 %collective-permute-start.16 = (f32[8,2,128]{2,0,1:T(8,128)S(1)}, f32[8,2,128]{2,0,1:T(8,128)S(1)}, u32[]{:S(2)}, u32[]{:S(2)}) collective-permute-start(f32[8,2,128]{2,0,1:T(8,128)S(1)} %get-tuple-element.23), channel_id=1, source_target_pairs={{1,0},{2,1},{3,2},{4,3},{5,4},{6,5},{7,6},{9,8},{10,9},{11,10},{12... | collective-permute-start | bytes 24584 | tf_op jit(solution)/shard_map/ppermute | solution.py:17
  91.0 2.7 %collective-permute-done.16 = f32[8,2,128]{2,0,1:T(8,128)S(1)} collective-permute-done((f32[8,2,128]{2,0,1:T(8,128)S(1)}, f32[8,2,128]{2,0,1:T(8,128)S(1)}, u32[]{:S(2)}, u32[]{:S(2)}) %collective-permute-start.16) | collective-permute-done | bytes 8224 | tf_op jit(solution)/shard_map/ppermute | solution.py:17
  94.4 3.4 %fusion.99 = f32[8,8,128]{2,0,1:T(8,128)S(1)} fusion(f32[8,8,128]{2,0,1:T(8,128)S(1)} %collective-permute-done.14, f32[8,8,4,128]{3,0,2,1:T(8,128)S(1)} %bitcast.298, f32[1,2,8,4,128,128]{5,4,3,2,1,0:T(8,128)} %param.8, f32[8,8,128]{2,1,0:T(8,128)S(1)} %copy-done.1, f32[8,128]{1,0:T(8,128)S(1)} %get-tuple-element.37, pred[]{:T(512)} %bitcast.2), kind=kOutput, calls=%fused_computation.71 | convolution fusion | flops 50356224 | bytes 2331136 | tf_op jit(solution)/shard_map/dbje,bjce->dbc/dot_general | solution.py:51
  97.8 1.9 collective-permute-start.17
  99.8 2.4 %collective-permute-start.18 = (f32[8,2,128]{2,0,1:T(8,128)S(1)}, f32[8,2,128]{2,0,1:T(8,128)S(1)}, u32[]{:S(2)}, u32[]{:S(2)}) collective-permute-start(f32[8,2,128]{2,0,1:T(8,128)S(1)} %get-tuple-element.21), channel_id=1, source_target_pairs={{1,0},{2,1},{3,2},{4,3},{5,4},{6,5},{7,6},{9,8},{10,9},{11,10},{12... | collective-permute-start | bytes 24584 | tf_op jit(solution)/shard_map/ppermute | solution.py:17
  102.2 2.6 %collective-permute-done.18 = f32[8,2,128]{2,0,1:T(8,128)S(1)} collective-permute-done((f32[8,2,128]{2,0,1:T(8,128)S(1)}, f32[8,2,128]{2,0,1:T(8,128)S(1)}, u32[]{:S(2)}, u32[]{:S(2)}) %collective-permute-start.18) | collective-permute-done | bytes 8224 | tf_op jit(solution)/shard_map/ppermute | solution.py:17
  105.5 3.5 %fusion.75 = f32[8,8,128]{2,0,1:T(8,128)S(1)} fusion(f32[8,8,128]{2,0,1:T(8,128)S(1)} %fusion.99, f32[8,8,4,128]{3,0,2,1:T(8,128)S(1)} %bitcast.299, f32[1,2,8,4,128,128]{5,4,3,2,1,0:T(8,128)} %param.8, f32[8,8,128]{2,1,0:T(8,128)S(1)} %copy-done.1, f32[8,128]{1,0:T(8,128)S(1)} %get-tuple-element.34, f32[8,128]{1,0:T(8,128)S(1)} %get-tuple-element.36, ...), kind=kOutput, calls=%fused_computation.63 | convolution fusion | flops 50364416 | bytes 2335232 | tf_op jit(solution)/shard_map/dbje,bjce->dbc/dot_general | solution.py:51
  109.0 2.7 %fusion.6 = f32[8,8,4,128]{3,1,2,0:T(8,128)S(1)} fusion(f32[1,2,8,4,128,128]{5,4,3,2,1,0:T(8,128)} %param.8, f32[8,8,128]{2,0,1:T(8,128)S(1)} %fusion.75), kind=kOutput, calls=%fused_computation.14 | convolution fusion | flops 50331648 | bytes 2260992 | tf_op jit(solution)/shard_map/dbc,bjce->dbje/dot_general | solution.py:74
  111.9 1.9 collective-permute-start.19
  113.9 2.4 %collective-permute-start.20 = (f32[8,2,128]{2,0,1:T(8,128)S(1)}, f32[8,2,128]{2,0,1:T(8,128)S(1)}, u32[]{:S(2)}, u32[]{:S(2)}) collective-permute-start(f32[8,2,128]{2,0,1:T(8,128)S(1)} %get-tuple-element.19), channel_id=1, source_target_pairs={{1,0},{2,1},{3,2},{4,3},{5,4},{6,5},{7,6},{9,8},{10,9},{11,10},{12... | collective-permute-start | bytes 24584 | tf_op jit(solution)/shard_map/ppermute | solution.py:17
  116.3 2.6 %collective-permute-done.20 = f32[8,2,128]{2,0,1:T(8,128)S(1)} collective-permute-done((f32[8,2,128]{2,0,1:T(8,128)S(1)}, f32[8,2,128]{2,0,1:T(8,128)S(1)}, u32[]{:S(2)}, u32[]{:S(2)}) %collective-permute-start.20) | collective-permute-done | bytes 8224 | tf_op jit(solution)/shard_map/ppermute | solution.py:17
  118.9 1.1 fusion.20
  120.2 1.9 collective-permute-start.21
  122.1 2.4 %collective-permute-start.22 = (f32[8,2,128]{2,0,1:T(8,128)S(1)}, f32[8,2,128]{2,0,1:T(8,128)S(1)}, u32[]{:S(2)}, u32[]{:S(2)}) collective-permute-start(f32[8,2,128]{2,0,1:T(8,128)S(1)} %get-tuple-element.17), channel_id=1, source_target_pairs={{1,0},{2,1},{3,2},{4,3},{5,4},{6,5},{7,6},{9,8},{10,9},{11,10},{12... | collective-permute-start | bytes 24584 | tf_op jit(solution)/shard_map/ppermute | solution.py:17
  124.5 2.6 %collective-permute-done.22 = f32[8,2,128]{2,0,1:T(8,128)S(1)} collective-permute-done((f32[8,2,128]{2,0,1:T(8,128)S(1)}, f32[8,2,128]{2,0,1:T(8,128)S(1)}, u32[]{:S(2)}, u32[]{:S(2)}) %collective-permute-start.22) | collective-permute-done | bytes 8224 | tf_op jit(solution)/shard_map/ppermute | solution.py:17
  127.1 1.3 collective-permute-start.23
  128.4 4.8 %collective-permute-done.23 = f32[8,8,128]{2,0,1:T(8,128)S(1)} collective-permute-done((f32[8,8,128]{2,0,1:T(8,128)S(1)}, f32[8,8,128]{2,0,1:T(8,128)S(1)}, u32[]{:S(2)}, u32[]{:S(2)}) %collective-permute-start.23) | collective-permute-done | bytes 32800 | tf_op jit(solution)/shard_map/ppermute | solution.py:25
  134.6 2.8 %collective-permute-start.24 = (f32[8,2,128]{2,0,1:T(8,128)S(1)}, f32[8,2,128]{2,0,1:T(8,128)S(1)}, u32[]{:S(2)}, u32[]{:S(2)}) collective-permute-start(f32[8,2,128]{2,0,1:T(8,128)S(1)} %get-tuple-element.14), channel_id=1, source_target_pairs={{0,1},{1,2},{2,3},{3,4},{4,5},{5,6},{6,7},{8,9},{9,10},{10,11},{11... | collective-permute-start | bytes 24584 | tf_op jit(solution)/shard_map/ppermute | solution.py:14
  137.4 1.9 collective-permute-start.25
  139.3 3.0 %collective-permute-done.25 = f32[8,2,128]{2,0,1:T(8,128)S(1)} collective-permute-done((f32[8,2,128]{2,0,1:T(8,128)S(1)}, f32[8,2,128]{2,0,1:T(8,128)S(1)}, u32[]{:S(2)}, u32[]{:S(2)}) %collective-permute-start.25) | collective-permute-done | bytes 8224 | tf_op jit(solution)/shard_map/ppermute | solution.py:17
  143.7 1.9 collective-permute-start.26
  145.6 2.4 %collective-permute-start.27 = (f32[8,2,128]{2,0,1:T(8,128)S(1)}, f32[8,2,128]{2,0,1:T(8,128)S(1)}, u32[]{:S(2)}, u32[]{:S(2)}) collective-permute-start(f32[8,2,128]{2,0,1:T(8,128)S(1)} %get-tuple-element.13), channel_id=1, source_target_pairs={{1,0},{2,1},{3,2},{4,3},{5,4},{6,5},{7,6},{9,8},{10,9},{11,10},{12... | collective-permute-start | bytes 24584 | tf_op jit(solution)/shard_map/ppermute | solution.py:17
  148.0 2.6 %collective-permute-done.27 = f32[8,2,128]{2,0,1:T(8,128)S(1)} collective-permute-done((f32[8,2,128]{2,0,1:T(8,128)S(1)}, f32[8,2,128]{2,0,1:T(8,128)S(1)}, u32[]{:S(2)}, u32[]{:S(2)}) %collective-permute-start.27) | collective-permute-done | bytes 8224 | tf_op jit(solution)/shard_map/ppermute | solution.py:17
  150.6 1.3 collective-permute-start.28
  151.9 4.8 %collective-permute-done.28 = f32[8,8,128]{2,0,1:T(8,128)S(1)} collective-permute-done((f32[8,8,128]{2,0,1:T(8,128)S(1)}, f32[8,8,128]{2,0,1:T(8,128)S(1)}, u32[]{:S(2)}, u32[]{:S(2)}) %collective-permute-start.28) | collective-permute-done | bytes 32800 | tf_op jit(solution)/shard_map/ppermute | solution.py:25
  158.1 2.8 %collective-permute-start.29 = (f32[8,2,128]{2,0,1:T(8,128)S(1)}, f32[8,2,128]{2,0,1:T(8,128)S(1)}, u32[]{:S(2)}, u32[]{:S(2)}) collective-permute-start(f32[8,2,128]{2,0,1:T(8,128)S(1)} %get-tuple-element.10), channel_id=1, source_target_pairs={{0,1},{1,2},{2,3},{3,4},{4,5},{5,6},{6,7},{8,9},{9,10},{10,11},{11... | collective-permute-start | bytes 24584 | tf_op jit(solution)/shard_map/ppermute | solution.py:14
  160.9 1.9 collective-permute-start.30
  162.9 3.0 %collective-permute-done.30 = f32[8,2,128]{2,0,1:T(8,128)S(1)} collective-permute-done((f32[8,2,128]{2,0,1:T(8,128)S(1)}, f32[8,2,128]{2,0,1:T(8,128)S(1)}, u32[]{:S(2)}, u32[]{:S(2)}) %collective-permute-start.30) | collective-permute-done | bytes 8224 | tf_op jit(solution)/shard_map/ppermute | solution.py:17
  167.2 1.9 collective-permute-start.31
  169.2 2.4 %collective-permute-start.32 = (f32[8,2,128]{2,0,1:T(8,128)S(1)}, f32[8,2,128]{2,0,1:T(8,128)S(1)}, u32[]{:S(2)}, u32[]{:S(2)}) collective-permute-start(f32[8,2,128]{2,0,1:T(8,128)S(1)} %get-tuple-element.9), channel_id=1, source_target_pairs={{1,0},{2,1},{3,2},{4,3},{5,4},{6,5},{7,6},{9,8},{10,9},{11,10},{12... | collective-permute-start | bytes 24584 | tf_op jit(solution)/shard_map/ppermute | solution.py:17
  171.6 2.6 %collective-permute-done.32 = f32[8,2,128]{2,0,1:T(8,128)S(1)} collective-permute-done((f32[8,2,128]{2,0,1:T(8,128)S(1)}, f32[8,2,128]{2,0,1:T(8,128)S(1)}, u32[]{:S(2)}, u32[]{:S(2)}) %collective-permute-start.32) | collective-permute-done | bytes 8224 | tf_op jit(solution)/shard_map/ppermute | solution.py:17
  174.1 1.3 collective-permute-start.33
  175.4 4.5 %collective-permute-done.33 = f32[8,8,128]{2,0,1:T(8,128)S(1)} collective-permute-done((f32[8,8,128]{2,0,1:T(8,128)S(1)}, f32[8,8,128]{2,0,1:T(8,128)S(1)}, u32[]{:S(2)}, u32[]{:S(2)}) %collective-permute-start.33) | collective-permute-done | bytes 32800 | tf_op jit(solution)/shard_map/ppermute | solution.py:25
  181.3 2.8 %collective-permute-start.34 = (f32[8,2,128]{2,0,1:T(8,128)S(1)}, f32[8,2,128]{2,0,1:T(8,128)S(1)}, u32[]{:S(2)}, u32[]{:S(2)}) collective-permute-start(f32[8,2,128]{2,0,1:T(8,128)S(1)} %get-tuple-element.6), channel_id=1, source_target_pairs={{0,1},{1,2},{2,3},{3,4},{4,5},{5,6},{6,7},{8,9},{9,10},{10,11},{11... | collective-permute-start | bytes 24584 | tf_op jit(solution)/shard_map/ppermute | solution.py:14
  184.1 1.9 collective-permute-start.35
  187.3 1.8 collective-permute-done.35
  189.1 13.2 %all-reduce.14 = f32[8,8,128]{2,1,0:T(8,128)S(1)} all-reduce(f32[8,8,128]{2,1,0:T(8,128)S(1)} %copy.66), channel_id=2, replica_groups=mesh['tm'=4,'map'=8] {'tm'}, use_global_device_ids=true, to_apply=%region_0.0.clone | all-reduce | flops 8192 | bytes 65536
  (110 shorter events, 19.4 us)
Async XLA Ops:
  0.0 38.6 %copy-start.1 = (f32[8,8,128]{2,1,0:T(8,128)S(1)}, f32[8,8,128]{2,1,0:T(8,128)}, u32[]{:S(2)}) copy-start(f32[8,8,128]{2,1,0:T(8,128)} %param.11) | copy-start | bytes 98308
  0.0 9.1 %collective-permute-start = (f32[8,2,128]{2,0,1:T(8,128)S(1)}, f32[8,2,128]{2,0,1:T(8,128)S(1)}, u32[]{:S(2)}, u32[]{:S(2)}) collective-permute-start(f32[8,2,128]{2,0,1:T(8,128)S(1)} %broadcast.45), channel_id=1, source_target_pairs={{0,1},{1,2},{2,3},{3,4},{4,5},{5,6},{6,7},{8,9},{9,10},{10,11},{11... | collective-permute-start | bytes 24584 | tf_op jit(solution)/shard_map/ppermute | solution.py:14
  4.7 5.0 %collective-permute-start.1 = (f32[8,2,128]{2,0,1:T(8,128)S(1)}, f32[8,2,128]{2,0,1:T(8,128)S(1)}, u32[]{:S(2)}, u32[]{:S(2)}) collective-permute-start(f32[8,2,128]{2,0,1:T(8,128)S(1)} %broadcast.45), channel_id=1, source_target_pairs={{1,0},{2,1},{3,2},{4,3},{5,4},{6,5},{7,6},{9,8},{10,9},{11,10},{12... | collective-permute-start | bytes 24584 | tf_op jit(solution)/shard_map/ppermute | solution.py:17
  13.8 5.0 %collective-permute-start.2 = (f32[8,2,128]{2,0,1:T(8,128)S(1)}, f32[8,2,128]{2,0,1:T(8,128)S(1)}, u32[]{:S(2)}, u32[]{:S(2)}) collective-permute-start(f32[8,2,128]{2,0,1:T(8,128)S(1)} %get-tuple-element.32), channel_id=1, source_target_pairs={{0,1},{1,2},{2,3},{3,4},{4,5},{5,6},{6,7},{8,9},{9,10},{10,11},{11... | collective-permute-start | bytes 24584 | tf_op jit(solution)/shard_map/ppermute | solution.py:14
  16.9 5.0 %collective-permute-start.3 = (f32[8,2,128]{2,0,1:T(8,128)S(1)}, f32[8,2,128]{2,0,1:T(8,128)S(1)}, u32[]{:S(2)}, u32[]{:S(2)}) collective-permute-start(f32[8,2,128]{2,0,1:T(8,128)S(1)} %get-tuple-element.33), channel_id=1, source_target_pairs={{1,0},{2,1},{3,2},{4,3},{5,4},{6,5},{7,6},{9,8},{10,9},{11,10},{12... | collective-permute-start | bytes 24584 | tf_op jit(solution)/shard_map/ppermute | solution.py:17
  26.0 4.1 %collective-permute-start.4 = (f32[8,8,128]{2,0,1:T(8,128)S(1)}, f32[8,8,128]{2,0,1:T(8,128)S(1)}, u32[]{:S(2)}, u32[]{:S(2)}) collective-permute-start(f32[8,8,128]{2,0,1:T(8,128)S(1)} %fusion.93), channel_id=1, source_target_pairs={{0,8},{8,16},{16,24},{1,9},{9,17},{17,25},{2,10},{10,18},{18,26},{... | collective-permute-start | bytes 98312 | tf_op jit(solution)/shard_map/ppermute | solution.py:25
  30.1 4.7 %collective-permute-start.5 = (f32[8,2,128]{2,0,1:T(8,128)S(1)}, f32[8,2,128]{2,0,1:T(8,128)S(1)}, u32[]{:S(2)}, u32[]{:S(2)}) collective-permute-start(f32[8,2,128]{2,0,1:T(8,128)S(1)} %get-tuple-element.30), channel_id=1, source_target_pairs={{0,1},{1,2},{2,3},{3,4},{4,5},{5,6},{6,7},{8,9},{9,10},{10,11},{11... | collective-permute-start | bytes 24584 | tf_op jit(solution)/shard_map/ppermute | solution.py:14
  32.9 5.0 %collective-permute-start.6 = (f32[8,2,128]{2,0,1:T(8,128)S(1)}, f32[8,2,128]{2,0,1:T(8,128)S(1)}, u32[]{:S(2)}, u32[]{:S(2)}) collective-permute-start(f32[8,2,128]{2,0,1:T(8,128)S(1)} %get-tuple-element.31), channel_id=1, source_target_pairs={{1,0},{2,1},{3,2},{4,3},{5,4},{6,5},{7,6},{9,8},{10,9},{11,10},{12... | collective-permute-start | bytes 24584 | tf_op jit(solution)/shard_map/ppermute | solution.py:17
  42.0 4.3 %collective-permute-start.7 = (f32[8,2,128]{2,0,1:T(8,128)S(1)}, f32[8,2,128]{2,0,1:T(8,128)S(1)}, u32[]{:S(2)}, u32[]{:S(2)}) collective-permute-start(f32[8,2,128]{2,0,1:T(8,128)S(1)} %get-tuple-element.28), channel_id=1, source_target_pairs={{0,1},{1,2},{2,3},{3,4},{4,5},{5,6},{6,7},{8,9},{9,10},{10,11},{11... | collective-permute-start | bytes 24584 | tf_op jit(solution)/shard_map/ppermute | solution.py:14
  44.0 5.0 %collective-permute-start.8 = (f32[8,2,128]{2,0,1:T(8,128)S(1)}, f32[8,2,128]{2,0,1:T(8,128)S(1)}, u32[]{:S(2)}, u32[]{:S(2)}) collective-permute-start(f32[8,2,128]{2,0,1:T(8,128)S(1)} %get-tuple-element.29), channel_id=1, source_target_pairs={{1,0},{2,1},{3,2},{4,3},{5,4},{6,5},{7,6},{9,8},{10,9},{11,10},{12... | collective-permute-start | bytes 24584 | tf_op jit(solution)/shard_map/ppermute | solution.py:17
  49.6 41.2 %copy-start.2 = (f32[1,2,8,128]{3,2,1,0:T(8,128)S(1)}, f32[1,2,8,128]{3,2,1,0:T(8,128)}, u32[]{:S(2)}) copy-start(f32[1,2,8,128]{3,2,1,0:T(8,128)} %param.13) | copy-start | bytes 24580
  53.0 5.0 %collective-permute-start.9 = (f32[8,8,128]{2,0,1:T(8,128)S(1)}, f32[8,8,128]{2,0,1:T(8,128)S(1)}, u32[]{:S(2)}, u32[]{:S(2)}) collective-permute-start(f32[8,8,128]{2,0,1:T(8,128)S(1)} %fusion.87), channel_id=1, source_target_pairs={{0,8},{8,16},{16,24},{1,9},{9,17},{17,25},{2,10},{10,18},{18,26},{... | collective-permute-start | bytes 98312 | tf_op jit(solution)/shard_map/ppermute | solution.py:25
  58.0 4.7 %collective-permute-start.10 = (f32[8,2,128]{2,0,1:T(8,128)S(1)}, f32[8,2,128]{2,0,1:T(8,128)S(1)}, u32[]{:S(2)}, u32[]{:S(2)}) collective-permute-start(f32[8,2,128]{2,0,1:T(8,128)S(1)} %get-tuple-element.26), channel_id=1, source_target_pairs={{0,1},{1,2},{2,3},{3,4},{4,5},{5,6},{6,7},{8,9},{9,10},{10,11},{11... | collective-permute-start | bytes 24584 | tf_op jit(solution)/shard_map/ppermute | solution.py:14
  60.8 5.0 %collective-permute-start.11 = (f32[8,2,128]{2,0,1:T(8,128)S(1)}, f32[8,2,128]{2,0,1:T(8,128)S(1)}, u32[]{:S(2)}, u32[]{:S(2)}) collective-permute-start(f32[8,2,128]{2,0,1:T(8,128)S(1)} %get-tuple-element.27), channel_id=1, source_target_pairs={{1,0},{2,1},{3,2},{4,3},{5,4},{6,5},{7,6},{9,8},{10,9},{11,10},{12... | collective-permute-start | bytes 24584 | tf_op jit(solution)/shard_map/ppermute | solution.py:17
  69.9 4.3 %collective-permute-start.12 = (f32[8,2,128]{2,0,1:T(8,128)S(1)}, f32[8,2,128]{2,0,1:T(8,128)S(1)}, u32[]{:S(2)}, u32[]{:S(2)}) collective-permute-start(f32[8,2,128]{2,0,1:T(8,128)S(1)} %get-tuple-element.24), channel_id=1, source_target_pairs={{0,1},{1,2},{2,3},{3,4},{4,5},{5,6},{6,7},{8,9},{9,10},{10,11},{11... | collective-permute-start | bytes 24584 | tf_op jit(solution)/shard_map/ppermute | solution.py:14
  71.8 5.0 %collective-permute-start.13 = (f32[8,2,128]{2,0,1:T(8,128)S(1)}, f32[8,2,128]{2,0,1:T(8,128)S(1)}, u32[]{:S(2)}, u32[]{:S(2)}) collective-permute-start(f32[8,2,128]{2,0,1:T(8,128)S(1)} %get-tuple-element.25), channel_id=1, source_target_pairs={{1,0},{2,1},{3,2},{4,3},{5,4},{6,5},{7,6},{9,8},{10,9},{11,10},{12... | collective-permute-start | bytes 24584 | tf_op jit(solution)/shard_map/ppermute | solution.py:17
  80.9 5.0 %collective-permute-start.14 = (f32[8,8,128]{2,0,1:T(8,128)S(1)}, f32[8,8,128]{2,0,1:T(8,128)S(1)}, u32[]{:S(2)}, u32[]{:S(2)}) collective-permute-start(f32[8,8,128]{2,0,1:T(8,128)S(1)} %fusion.81), channel_id=1, source_target_pairs={{0,8},{8,16},{16,24},{1,9},{9,17},{17,25},{2,10},{10,18},{18,26},{... | collective-permute-start | bytes 98312 | tf_op jit(solution)/shard_map/ppermute | solution.py:25
  85.9 5.1 %collective-permute-start.15 = (f32[8,2,128]{2,0,1:T(8,128)S(1)}, f32[8,2,128]{2,0,1:T(8,128)S(1)}, u32[]{:S(2)}, u32[]{:S(2)}) collective-permute-start(f32[8,2,128]{2,0,1:T(8,128)S(1)} %get-tuple-element.22), channel_id=1, source_target_pairs={{0,1},{1,2},{2,3},{3,4},{4,5},{5,6},{6,7},{8,9},{9,10},{10,11},{11... | collective-permute-start | bytes 24584 | tf_op jit(solution)/shard_map/ppermute | solution.py:14
  88.7 5.0 %collective-permute-start.16 = (f32[8,2,128]{2,0,1:T(8,128)S(1)}, f32[8,2,128]{2,0,1:T(8,128)S(1)}, u32[]{:S(2)}, u32[]{:S(2)}) collective-permute-start(f32[8,2,128]{2,0,1:T(8,128)S(1)} %get-tuple-element.23), channel_id=1, source_target_pairs={{1,0},{2,1},{3,2},{4,3},{5,4},{6,5},{7,6},{9,8},{10,9},{11,10},{12... | collective-permute-start | bytes 24584 | tf_op jit(solution)/shard_map/ppermute | solution.py:17
  97.8 4.4 %collective-permute-start.17 = (f32[8,2,128]{2,0,1:T(8,128)S(1)}, f32[8,2,128]{2,0,1:T(8,128)S(1)}, u32[]{:S(2)}, u32[]{:S(2)}) collective-permute-start(f32[8,2,128]{2,0,1:T(8,128)S(1)} %get-tuple-element.20), channel_id=1, source_target_pairs={{0,1},{1,2},{2,3},{3,4},{4,5},{5,6},{6,7},{8,9},{9,10},{10,11},{11... | collective-permute-start | bytes 24584 | tf_op jit(solution)/shard_map/ppermute | solution.py:14
  99.8 5.0 %collective-permute-start.18 = (f32[8,2,128]{2,0,1:T(8,128)S(1)}, f32[8,2,128]{2,0,1:T(8,128)S(1)}, u32[]{:S(2)}, u32[]{:S(2)}) collective-permute-start(f32[8,2,128]{2,0,1:T(8,128)S(1)} %get-tuple-element.21), channel_id=1, source_target_pairs={{1,0},{2,1},{3,2},{4,3},{5,4},{6,5},{7,6},{9,8},{10,9},{11,10},{12... | collective-permute-start | bytes 24584 | tf_op jit(solution)/shard_map/ppermute | solution.py:17
  105.3 13.5 %copy-start = (f32[1,2,8,4,128,128]{5,4,3,2,1,0:T(8,128)S(1)}, f32[1,2,8,4,128,128]{5,4,3,2,1,0:T(8,128)}, u32[]{:S(2)}) copy-start(f32[1,2,8,4,128,128]{5,4,3,2,1,0:T(8,128)} %param.8) | copy-start | bytes 12582916
  111.9 4.3 %collective-permute-start.19 = (f32[8,2,128]{2,0,1:T(8,128)S(1)}, f32[8,2,128]{2,0,1:T(8,128)S(1)}, u32[]{:S(2)}, u32[]{:S(2)}) collective-permute-start(f32[8,2,128]{2,0,1:T(8,128)S(1)} %get-tuple-element.18), channel_id=1, source_target_pairs={{0,1},{1,2},{2,3},{3,4},{4,5},{5,6},{6,7},{8,9},{9,10},{10,11},{11... | collective-permute-start | bytes 24584 | tf_op jit(solution)/shard_map/ppermute | solution.py:14
  113.9 5.0 %collective-permute-start.20 = (f32[8,2,128]{2,0,1:T(8,128)S(1)}, f32[8,2,128]{2,0,1:T(8,128)S(1)}, u32[]{:S(2)}, u32[]{:S(2)}) collective-permute-start(f32[8,2,128]{2,0,1:T(8,128)S(1)} %get-tuple-element.19), channel_id=1, source_target_pairs={{1,0},{2,1},{3,2},{4,3},{5,4},{6,5},{7,6},{9,8},{10,9},{11,10},{12... | collective-permute-start | bytes 24584 | tf_op jit(solution)/shard_map/ppermute | solution.py:17
  120.2 4.3 %collective-permute-start.21 = (f32[8,2,128]{2,0,1:T(8,128)S(1)}, f32[8,2,128]{2,0,1:T(8,128)S(1)}, u32[]{:S(2)}, u32[]{:S(2)}) collective-permute-start(f32[8,2,128]{2,0,1:T(8,128)S(1)} %get-tuple-element.16), channel_id=1, source_target_pairs={{0,1},{1,2},{2,3},{3,4},{4,5},{5,6},{6,7},{8,9},{9,10},{10,11},{11... | collective-permute-start | bytes 24584 | tf_op jit(solution)/shard_map/ppermute | solution.py:14
  122.1 5.0 %collective-permute-start.22 = (f32[8,2,128]{2,0,1:T(8,128)S(1)}, f32[8,2,128]{2,0,1:T(8,128)S(1)}, u32[]{:S(2)}, u32[]{:S(2)}) collective-permute-start(f32[8,2,128]{2,0,1:T(8,128)S(1)} %get-tuple-element.17), channel_id=1, source_target_pairs={{1,0},{2,1},{3,2},{4,3},{5,4},{6,5},{7,6},{9,8},{10,9},{11,10},{12... | collective-permute-start | bytes 24584 | tf_op jit(solution)/shard_map/ppermute | solution.py:17
  127.1 6.1 %collective-permute-start.23 = (f32[8,8,128]{2,0,1:T(8,128)S(1)}, f32[8,8,128]{2,0,1:T(8,128)S(1)}, u32[]{:S(2)}, u32[]{:S(2)}) collective-permute-start(f32[8,8,128]{2,0,1:T(8,128)S(1)} %fusion.149), channel_id=1, source_target_pairs={{8,0},{16,8},{24,16},{9,1},{17,9},{25,17},{10,2},{18,10},{26,18},{... | collective-permute-start | bytes 98312 | tf_op jit(solution)/shard_map/ppermute | solution.py:25
  134.6 4.8 %collective-permute-start.24 = (f32[8,2,128]{2,0,1:T(8,128)S(1)}, f32[8,2,128]{2,0,1:T(8,128)S(1)}, u32[]{:S(2)}, u32[]{:S(2)}) collective-permute-start(f32[8,2,128]{2,0,1:T(8,128)S(1)} %get-tuple-element.14), channel_id=1, source_target_pairs={{0,1},{1,2},{2,3},{3,4},{4,5},{5,6},{6,7},{8,9},{9,10},{10,11},{11... | collective-permute-start | bytes 24584 | tf_op jit(solution)/shard_map/ppermute | solution.py:14
  137.4 5.0 %collective-permute-start.25 = (f32[8,2,128]{2,0,1:T(8,128)S(1)}, f32[8,2,128]{2,0,1:T(8,128)S(1)}, u32[]{:S(2)}, u32[]{:S(2)}) collective-permute-start(f32[8,2,128]{2,0,1:T(8,128)S(1)} %get-tuple-element.15), channel_id=1, source_target_pairs={{1,0},{2,1},{3,2},{4,3},{5,4},{6,5},{7,6},{9,8},{10,9},{11,10},{12... | collective-permute-start | bytes 24584 | tf_op jit(solution)/shard_map/ppermute | solution.py:17
  143.7 42.4 %copy-start.3 = (u32[32]{0:T(128)S(1)}, u32[32]{0:T(128)}, u32[]{:S(2)}) copy-start(u32[32]{0:T(128)} %constant.65) | copy-start | bytes 388
  143.7 4.3 %collective-permute-start.26 = (f32[8,2,128]{2,0,1:T(8,128)S(1)}, f32[8,2,128]{2,0,1:T(8,128)S(1)}, u32[]{:S(2)}, u32[]{:S(2)}) collective-permute-start(f32[8,2,128]{2,0,1:T(8,128)S(1)} %get-tuple-element.12), channel_id=1, source_target_pairs={{0,1},{1,2},{2,3},{3,4},{4,5},{5,6},{6,7},{8,9},{9,10},{10,11},{11... | collective-permute-start | bytes 24584 | tf_op jit(solution)/shard_map/ppermute | solution.py:14
  145.6 5.0 %collective-permute-start.27 = (f32[8,2,128]{2,0,1:T(8,128)S(1)}, f32[8,2,128]{2,0,1:T(8,128)S(1)}, u32[]{:S(2)}, u32[]{:S(2)}) collective-permute-start(f32[8,2,128]{2,0,1:T(8,128)S(1)} %get-tuple-element.13), channel_id=1, source_target_pairs={{1,0},{2,1},{3,2},{4,3},{5,4},{6,5},{7,6},{9,8},{10,9},{11,10},{12... | collective-permute-start | bytes 24584 | tf_op jit(solution)/shard_map/ppermute | solution.py:17
  150.6 6.1 %collective-permute-start.28 = (f32[8,8,128]{2,0,1:T(8,128)S(1)}, f32[8,8,128]{2,0,1:T(8,128)S(1)}, u32[]{:S(2)}, u32[]{:S(2)}) collective-permute-start(f32[8,8,128]{2,0,1:T(8,128)S(1)} %fusion.145), channel_id=1, source_target_pairs={{8,0},{16,8},{24,16},{9,1},{17,9},{25,17},{10,2},{18,10},{26,18},{... | collective-permute-start | bytes 98312 | tf_op jit(solution)/shard_map/ppermute | solution.py:25
  158.1 4.8 %collective-permute-start.29 = (f32[8,2,128]{2,0,1:T(8,128)S(1)}, f32[8,2,128]{2,0,1:T(8,128)S(1)}, u32[]{:S(2)}, u32[]{:S(2)}) collective-permute-start(f32[8,2,128]{2,0,1:T(8,128)S(1)} %get-tuple-element.10), channel_id=1, source_target_pairs={{0,1},{1,2},{2,3},{3,4},{4,5},{5,6},{6,7},{8,9},{9,10},{10,11},{11... | collective-permute-start | bytes 24584 | tf_op jit(solution)/shard_map/ppermute | solution.py:14
  160.9 5.0 %collective-permute-start.30 = (f32[8,2,128]{2,0,1:T(8,128)S(1)}, f32[8,2,128]{2,0,1:T(8,128)S(1)}, u32[]{:S(2)}, u32[]{:S(2)}) collective-permute-start(f32[8,2,128]{2,0,1:T(8,128)S(1)} %get-tuple-element.11), channel_id=1, source_target_pairs={{1,0},{2,1},{3,2},{4,3},{5,4},{6,5},{7,6},{9,8},{10,9},{11,10},{12... | collective-permute-start | bytes 24584 | tf_op jit(solution)/shard_map/ppermute | solution.py:17
  167.2 4.3 %collective-permute-start.31 = (f32[8,2,128]{2,0,1:T(8,128)S(1)}, f32[8,2,128]{2,0,1:T(8,128)S(1)}, u32[]{:S(2)}, u32[]{:S(2)}) collective-permute-start(f32[8,2,128]{2,0,1:T(8,128)S(1)} %get-tuple-element.8), channel_id=1, source_target_pairs={{0,1},{1,2},{2,3},{3,4},{4,5},{5,6},{6,7},{8,9},{9,10},{10,11},{11... | collective-permute-start | bytes 24584 | tf_op jit(solution)/shard_map/ppermute | solution.py:14
  169.2 5.0 %collective-permute-start.32 = (f32[8,2,128]{2,0,1:T(8,128)S(1)}, f32[8,2,128]{2,0,1:T(8,128)S(1)}, u32[]{:S(2)}, u32[]{:S(2)}) collective-permute-start(f32[8,2,128]{2,0,1:T(8,128)S(1)} %get-tuple-element.9), channel_id=1, source_target_pairs={{1,0},{2,1},{3,2},{4,3},{5,4},{6,5},{7,6},{9,8},{10,9},{11,10},{12... | collective-permute-start | bytes 24584 | tf_op jit(solution)/shard_map/ppermute | solution.py:17
  174.1 5.8 %collective-permute-start.33 = (f32[8,8,128]{2,0,1:T(8,128)S(1)}, f32[8,8,128]{2,0,1:T(8,128)S(1)}, u32[]{:S(2)}, u32[]{:S(2)}) collective-permute-start(f32[8,8,128]{2,0,1:T(8,128)S(1)} %fusion.141), channel_id=1, source_target_pairs={{8,0},{16,8},{24,16},{9,1},{17,9},{25,17},{10,2},{18,10},{26,18},{... | collective-permute-start | bytes 98312 | tf_op jit(solution)/shard_map/ppermute | solution.py:25
  181.3 6.0 %collective-permute-start.34 = (f32[8,2,128]{2,0,1:T(8,128)S(1)}, f32[8,2,128]{2,0,1:T(8,128)S(1)}, u32[]{:S(2)}, u32[]{:S(2)}) collective-permute-start(f32[8,2,128]{2,0,1:T(8,128)S(1)} %get-tuple-element.6), channel_id=1, source_target_pairs={{0,1},{1,2},{2,3},{3,4},{4,5},{5,6},{6,7},{8,9},{9,10},{10,11},{11... | collective-permute-start | bytes 24584 | tf_op jit(solution)/shard_map/ppermute | solution.py:14
  184.1 5.0 %collective-permute-start.35 = (f32[8,2,128]{2,0,1:T(8,128)S(1)}, f32[8,2,128]{2,0,1:T(8,128)S(1)}, u32[]{:S(2)}, u32[]{:S(2)}) collective-permute-start(f32[8,2,128]{2,0,1:T(8,128)S(1)} %get-tuple-element.7), channel_id=1, source_target_pairs={{1,0},{2,1},{3,2},{4,3},{5,4},{6,5},{7,6},{9,8},{10,9},{11,10},{12... | collective-permute-start | bytes 24584 | tf_op jit(solution)/shard_map/ppermute | solution.py:17
where the time goes:
time: 206 us; the launch traced here: 203 us
  starting transfers between devices  85.4 us (41%)
  waiting for transfers between devices  55.5 us (27%)
  matrix products  37.9 us (18%)
  blocking collectives  13.2 us (6%)
  local copies, waits for them, and re-layouts  7.32 us (4%)
    ppermute x15, starting transfers between devices, extended_2(): lax.ppermute(lax.slice_in_dim(block, block.shape[dim] - width, None, axis...  38.2 us
    ppermute x15, waiting for transfers between devices, extended_2(): lax.ppermute(lax.slice_in_dim(block, 0, width, axis=dim), axis, backward)  38.2 us
    ppermute x15, starting transfers between devices, extended_2(): lax.ppermute(lax.slice_in_dim(block, 0, width, axis=dim), axis, backward)  32.2 us
    dot_general x8, matrix products, shards(): jnp.einsum('dbje,bjce->dbc', picked, tiles[0, forward_step_index], precis...  27.3 us
    ppermute x6, waiting for transfers between devices, from_behind(): lax.ppermute(value, axis, [(source, source + steps) for source in range(l...  17.2 us
    ppermute x6, starting transfers between devices, from_behind(): lax.ppermute(value, axis, [(source, source + steps) for source in range(l...  15 us
    unnamed x1, blocking collectives  13.2 us
    dot_general x7, matrix products, shards(): jnp.einsum('dbc,bjce->dbje', adjoint, tiles[0, step_index], precision=lax...  9.3 us
  transfers between devices with their start and end apart: 36, of which 21 were waited for; matrix products, arithmetic and copies ran while one was open for 1% of the time, Pallas kernels for 0%

commit v1 on v0

v1 whole, which is shorter than its diff:
```python
import functools

import jax
import jax.numpy as jnp
from jax import lax
from jax.experimental import pallas as pl
from jax.experimental.pallas import tpu as pltpu
from jax.sharding import PartitionSpec as P

HALO = 2
MESH = pl.DeviceIdType.MESH
F32 = jnp.float32
BF16 = jnp.bfloat16


def split(x):
    high = x.astype(BF16).astype(F32)
    return jnp.concatenate([high, x - high], axis=0).astype(BF16)


def kernel(
    windows,
    parts,
    tiles,
    columns,
    steps,
    direction,
    forcing,
    observe,
    out,
    raw,
    weights,
    ext0,
    ext1,
    state1,
    state2,
    fin,
    fhalo,
    bin_core,
    bin_rim,
    bhalo,
    brim_out,
    bcore_out,
    brim_out0,
    grad_out,
    grad_in,
    load_sem,
    fwd_send,
    fwd_recv,
    fh_send,
    fh_recv,
    bwd_send,
    bwd_recv,
    bh_send,
    bh_recv,
    g_send,
    g_recv,
):
    dirs, nb, tile = direction.shape
    slots = columns.shape[3]
    width = nb + 2 * HALO
    dpw = dirs // windows
    w = lax.axis_index("tm")
    p = lax.axis_index("map")
    has_prev, has_next = w > 0, w < windows - 1
    has_lo, has_hi = p > 0, p < parts - 1

    loads = [
        pltpu.make_async_copy(tiles.at[0, k], raw.at[k], load_sem.at[k]) for k in range(2)
    ]
    for load in loads:
        load.start()
    for ref in (fin, fhalo, bin_core, bin_rim, bhalo):
        ref[...] = jnp.zeros(ref.shape, F32)

    barrier = pltpu.get_barrier_semaphore()
    count = jnp.int32(0)
    for dw in (-1, 0, 1):
        for dp in (-1, 0, 1):
            if dp == 0:
                continue
            ok = (w + dw >= 0) & (w + dw < windows) & (p + dp >= 0) & (p + dp < parts)

            @pl.when(ok)
            def _():
                pl.semaphore_signal(
                    barrier, inc=1, device_id={"tm": w + dw, "map": p + dp}, device_id_type=MESH
                )

            count = count + ok.astype(jnp.int32)
    for o in range(1, windows):
        pl.semaphore_signal(
            barrier, inc=1, device_id={"tm": lax.rem(w + o, windows)}, device_id_type=MESH
        )
    count = count + (windows - 1)

    first = p * nb - HALO
    local = [
        [
            [jnp.clip(columns[0, k, b, j] - first, 0, width - 1) for j in range(slots)]
            for b in range(nb)
        ]
        for k in range(2)
    ]
    active = [jnp.full((dirs, tile), steps[0], jnp.int32) > k for k in range(2)]

    def convert(k):
        def row(b, carry):
            for j in range(slots):
                x = raw[k, b, j]
                high = x.astype(BF16)
                weights[k, b, :tile, j * tile : (j + 1) * tile] = high
                weights[k, b, tile:, j * tile : (j + 1) * tile] = (
                    x - high.astype(F32)
                ).astype(BF16)
            return carry

        lax.fori_loop(0, nb, row, 0)

    pending = []

    def send(ok, src, dst, send_sem, recv_sem, target):
        copy = pltpu.make_async_remote_copy(
            src_ref=src,
            dst_ref=dst,
            send_sem=send_sem,
            recv_sem=recv_sem,
            device_id=target,
            device_id_type=MESH,
        )

        @pl.when(ok)
        def _():
            copy.start()

        pending.append((ok, copy))

    def arrived(ok, dst, send_sem, recv_sem):
        copy = pltpu.make_async_remote_copy(
            src_ref=dst,
            dst_ref=dst,
            send_sem=send_sem,
            recv_sem=recv_sem,
            device_id={"tm": w, "map": p},
            device_id_type=MESH,
        )

        @pl.when(ok)
        def _():
            copy.wait_recv()

    chunks = ((0, HALO), (nb - HALO, HALO), (HALO, nb - 2 * HALO))
    order = [*range(HALO), *range(nb - HALO, nb), *range(HALO, nb - HALO)]
    low, high_at = slice(0, HALO), slice(HALO, 2 * HALO)

    load_rows = [direction[:, b, :] for b in range(nb)]
    loads[0].wait()
    convert(0)
    loads[1].wait()
    convert(1)

    def product(k, ext, b):
        lhs = jnp.concatenate([ext[local[k][b][j]] for j in range(slots)], axis=1)
        r = lax.dot_general(
            lhs, weights[k, b], (((1,), (1,)), ((), ())), preferred_element_type=F32
        )
        r = r[:dirs] + r[dirs:]
        return r[:, :tile] + r[:, tile:]

    for i, (start, size) in enumerate(chunks):
        arrived(has_prev, fin.at[pl.ds(HALO + start, size)], fwd_send.at[i], fwd_recv.at[i])
    arrived(has_prev & has_lo, fin.at[pl.ds(0, HALO)], fwd_send.at[3], fwd_recv.at[3])
    arrived(
        has_prev & has_hi, fin.at[pl.ds(HALO + nb, HALO)], fwd_send.at[4], fwd_recv.at[4]
    )
    for q in range(width):
        ext0[q] = split(fin[q])
    for n, b in enumerate(order):
        new = product(0, ext0, b) + forcing[0, 0, b : b + 1] * load_rows[b]
        new = jnp.where(active[0], new, fin[HALO + b])
        state1[b] = new
        ext1[HALO + b] = split(new)
        if n == 2 * HALO - 1:
            pl.semaphore_wait(barrier, count)
            send(
                has_lo,
                state1.at[pl.ds(0, HALO)],
                fhalo.at[high_at],
                fh_send.at[0],
                fh_recv.at[0],
                {"tm": w, "map": p - 1},
            )
            send(
                has_hi,
                state1.at[pl.ds(nb - HALO, HALO)],
                fhalo.at[low],
                fh_send.at[1],
                fh_recv.at[1],
                {"tm": w, "map": p + 1},
            )
    arrived(has_hi, fhalo.at[high_at], fh_send.at[0], fh_recv.at[0])
    arrived(has_lo, fhalo.at[low], fh_send.at[1], fh_recv.at[1])
    for q in range(HALO):
        ext1[q] = split(fhalo[q])
        ext1[HALO + nb + q] = split(fhalo[HALO + q])
    for n, b in enumerate(order):
        new = product(1, ext1, b) + forcing[0, 1, b : b + 1] * load_rows[b]
        state2[b] = jnp.where(active[1], new, state1[b])
        if n == HALO - 1:
            send(
                has_next & has_lo,
                state2.at[pl.ds(0, HALO)],
                fin.at[pl.ds(HALO + nb, HALO)],
                fwd_send.at[4],
                fwd_recv.at[4],
                {"tm": w + 1, "map": p - 1},
            )
        if n == 2 * HALO - 1:
            send(
                has_next & has_hi,
                state2.at[pl.ds(nb - HALO, HALO)],
                fin.at[pl.ds(0, HALO)],
                fwd_send.at[3],
                fwd_recv.at[3],
                {"tm": w + 1, "map": p + 1},
            )
        for i, (start, size) in enumerate(chunks):
            if n == (HALO - 1, 2 * HALO - 1, nb - 1)[i]:
                send(
                    has_next,
                    state2.at[pl.ds(start, size)],
                    fin.at[pl.ds(HALO + start, size)],
                    fwd_send.at[i],
                    fwd_recv.at[i],
                    {"tm": w + 1, "map": p},
                )

    def scatter(k, b, a, spread):
        s = split(a)
        r = lax.dot_general(
            jnp.concatenate([s, s], axis=1),
            weights[k, b],
            (((1,), (0,)), ((), ())),
            preferred_element_type=F32,
        )
        r = r[:dirs] + r[dirs:]
        for j in range(slots):
            at = jnp.full((dirs, tile), local[k][b][j], jnp.int32)
            part = r[:, j * tile : (j + 1) * tile]
            for q in range(width):
                spread[q] = spread[q] + jnp.where(at == q, part, 0.0)

    seen1 = [observe[0, 1, b : b + 1] * state2[b] for b in range(nb)]
    arrived(has_next, bin_core, bwd_send.at[0], bwd_recv.at[0])
    arrived(has_next & has_lo, bin_rim.at[low], bwd_send.at[1], bwd_recv.at[1])
    arrived(has_next & has_hi, bin_rim.at[high_at], bwd_send.at[2], bwd_recv.at[2])
    carried = [bin_core[b] for b in range(nb)]
    for q in range(HALO):
        carried[q] = carried[q] + bin_rim[q]
        carried[nb - HALO + q] = carried[nb - HALO + q] + bin_rim[HALO + q]
    zero = jnp.zeros((dirs, tile), F32)
    spread = [zero] * width
    gradient = [None] * nb
    for b in range(nb):
        a = carried[b] + seen1[b]
        gradient[b] = jnp.where(active[1], forcing[0, 1, b : b + 1] * a, 0.0)
        scatter(1, b, a, spread)
    for q in range(HALO):
        brim_out[q] = spread[q]
        brim_out[HALO + q] = spread[HALO + nb + q]
    send(
        has_lo,
        brim_out.at[low],
        bhalo.at[high_at],
        bh_send.at[0],
        bh_recv.at[0],
        {"tm": w, "map": p - 1},
    )
    send(
        has_hi,
        brim_out.at[high_at],
        bhalo.at[low],
        bh_send.at[1],
        bh_recv.at[1],
        {"tm": w, "map": p + 1},
    )
    inner = spread[HALO : HALO + nb]
    spread = [zero] * width
    after1 = list(carried)
    for n, b in enumerate([*range(HALO, nb - HALO), *range(HALO), *range(nb - HALO, nb)]):
        if n == nb - 2 * HALO:
            arrived(has_hi, bhalo.at[high_at], bh_send.at[0], bh_recv.at[0])
            arrived(has_lo, bhalo.at[low], bh_send.at[1], bh_recv.at[1])
        value = inner[b]
        if b < HALO:
            value = value + bhalo[b]
        if b >= nb - HALO:
            value = value + bhalo[HALO + b - (nb - HALO)]
        value = jnp.where(active[1], value, carried[b])
        after1[b] = value
        a = value + observe[0, 0, b : b + 1] * state1[b]
        gradient[b] = gradient[b] + jnp.where(
            active[0], forcing[0, 0, b : b + 1] * a, 0.0
        )
        scatter(0, b, a, spread)
    for q in range(HALO):
        brim_out0[q] = jnp.where(active[0], spread[q], 0.0)
        brim_out0[HALO + q] = jnp.where(active[0], spread[HALO + nb + q], 0.0)
    for b in range(nb):
        bcore_out[b] = jnp.where(active[0], spread[HALO + b], after1[b])
    send(
        has_prev & has_lo,
        brim_out0.at[low],
        bin_rim.at[high_at],
        bwd_send.at[2],
        bwd_recv.at[2],
        {"tm": w - 1, "map": p - 1},
    )
    send(
        has_prev & has_hi,
        brim_out0.at[high_at],
        bin_rim.at[low],
        bwd_send.at[1],
        bwd_recv.at[1],
        {"tm": w - 1, "map": p + 1},
    )
    send(
        has_prev,
        bcore_out,
        bin_core,
        bwd_send.at[0],
        bwd_recv.at[0],
        {"tm": w - 1, "map": p},
    )

    for b in range(nb):
        grad_out[:, b, :] = gradient[b]
    always = w >= 0
    for o in range(1, windows):
        target = lax.rem(w + o, windows)
        send(
            always,
            grad_out.at[pl.ds(target * dpw, dpw)],
            grad_in.at[o - 1],
            g_send.at[o - 1],
            g_recv.at[o - 1],
            {"tm": target, "map": p},
        )
    total = grad_out[pl.ds(w * dpw, dpw)]
    for o in range(1, windows):
        arrived(always, grad_in.at[o - 1], g_send.at[o - 1], g_recv.at[o - 1])
        total = total + grad_in[o - 1]
    out[...] = total
    for ok, copy in pending:

        @pl.when(ok)
        def _():
            copy.wait_send()


def shards(windows, parts, tiles, columns, window_steps, direction, forcing, observe):
    dirs, nb, tile = direction.shape
    slots = tiles.shape[3]
    width = nb + 2 * HALO
    dpw = dirs // windows
    vmem = pl.BlockSpec(memory_space=pltpu.VMEM)
    smem = pl.BlockSpec(memory_space=pltpu.SMEM)
    block = lambda *lead: pltpu.VMEM((*lead, dirs, tile), F32)
    sems = lambda n: pltpu.SemaphoreType.DMA((n,))
    return pl.pallas_call(
        functools.partial(kernel, windows, parts),
        out_shape=jax.ShapeDtypeStruct((dpw, nb, tile), F32),
        in_specs=[pl.BlockSpec(memory_space=pl.ANY), smem, smem, vmem, vmem, vmem],
        out_specs=vmem,
        scratch_shapes=[
            pltpu.VMEM((2, nb, slots, tile, tile), F32),
            pltpu.VMEM((2, nb, 2 * tile, slots * tile), BF16),
            pltpu.VMEM((width, 2 * dirs, tile), BF16),
            pltpu.VMEM((width, 2 * dirs, tile), BF16),
            block(nb),
            block(nb),
            block(width),
            block(2 * HALO),
            block(nb),
            block(2 * HALO),
            block(2 * HALO),
            block(2 * HALO),
            block(nb),
            block(2 * HALO),
            pltpu.VMEM((dirs, nb, tile), F32),
            pltpu.VMEM((windows - 1, dpw, nb, tile), F32),
            sems(2),
            sems(5),
            sems(5),
            sems(2),
            sems(2),
            sems(3),
            sems(3),
            sems(2),
            sems(2),
            sems(windows - 1),
            sems(windows - 1),
        ],
        compiler_params=pltpu.CompilerParams(
            collective_id=0, has_side_effects=True, vmem_limit_bytes=32 * 1024 * 1024
        ),
    )(tiles, columns, window_steps, direction, forcing, observe)


def solution(mesh):
    placed = (
        P("tm", None, "map", None, None, None),
        P("tm", None, "map", None),
        P("tm"),
        P(None, "map", None),
        P("tm", None, "map", None),
        P("tm", None, "map", None),
    )
    return jax.shard_map(
        functools.partial(shards, mesh.shape["tm"], mesh.shape["map"]),
        mesh=mesh,
        in_specs=placed,
        out_specs=P("tm", "map", None),
        check_vma=False,
    )
```

time: 206 us -> 55.3 us (0.27); the launches traced: 203 us -> 55 us
  starting transfers between devices: 85.4 us -> 0 us
  waiting for transfers between devices: 55.5 us -> 0 us
  Pallas kernels: 0 us -> 48.6 us
  matrix products: 37.9 us -> 0 us
  blocking collectives: 13.2 us -> 0 us
    ppermute x36 -> x0, starting transfers between devices: 85.4 us -> none  [the longest x15 38.2 us: extended_2(): lax.ppermute(lax.slice_in_dim(block, block.shape[dim] - width, None, axis...]
    ppermute x36 -> x0, waiting for transfers between devices: 55.5 us -> none  [the longest x15 38.2 us: extended_2(): lax.ppermute(lax.slice_in_dim(block, 0, width, axis=dim), axis, backward)]
    pallas_call x0 -> x1, Pallas kernels: none -> 48.6 us  [shards(): pl.pallas_call(functools.partial(kernel, windows, parts), out_shape=jax.S...]
    dot_general x22 -> x0, matrix products: 37.9 us -> none  [the longest x8 27.3 us: shards(): jnp.einsum('dbje,bjce->dbc', picked, tiles[0, forward_step_index], precis...]
    unnamed x1 -> x0, blocking collectives: 13.2 us -> none
    gather x8 -> x0, local copies, waits for them, and re-layouts: 4.67 us -> none  [shards(): jnp.take(extended, local_cols[forward_step_index].reshape(-1), axis=1)]
    unnamed x10, local copies, waits for them, and re-layouts: 1.24 us -> 5.71 us
  transfers between devices with their start and end apart: 36 -> 0, of which waited for: 21 -> 0; matrix products, arithmetic and copies ran while one was open for 1% -> 0% of each run, Pallas kernels for 0% -> 0%
where the time goes in v1:
time: 55.3 us; the launch traced here: 55 us
  Pallas kernels  48.6 us (88%)
  local copies, waits for them, and re-layouts  5.71 us (10%)
  between operations  0.67 us (1%)
    pallas_call x1, Pallas kernels, shards(): pl.pallas_call(functools.partial(kernel, windows, parts), out_shape=jax.S...  48.6 us
    unnamed x10, local copies, waits for them, and re-layouts  5.71 us

profile of v1, /device:TPU:1, one launch (start us, length us, event | category | flops | bytes accessed | tf_op | source)
XLA Modules:
  0.0 55.0 jit_solution(6265605264877133463)
XLA Ops:
  0.7 0.8 %copy.7.columns = s32[1,2,8,4]{3,2,1,0:T(8,128)S(1)} copy(s32[1,2,8,4]{2,3,1,0:T(4,128)} %param.7) | data formatting | bytes 512 | tf_op args[1]
  1.4 0.0 copy-start
  1.4 2.2 %copy-done = f32[1,2,8,4,128,128]{5,4,3,2,1,0:T(8,128)S(1)} copy-done((f32[1,2,8,4,128,128]{5,4,3,2,1,0:T(8,128)S(1)}, f32[1,2,8,4,128,128]{5,4,3,2,1,0:T(8,128)}, u32[]{:S(2)}) %copy-start) | copy-done | bytes 4194328
  3.6 0.0 copy-start.1
  3.6 0.8 %copy-done.1 = f32[8,8,128]{2,1,0:T(8,128)S(1)} copy-done((f32[8,8,128]{2,1,0:T(8,128)S(1)}, f32[8,8,128]{2,1,0:T(8,128)}, u32[]{:S(2)}) %copy-start.1) | copy-done | bytes 32792
  4.4 0.0 copy-start.2
  4.4 0.7 %copy-done.2 = f32[1,2,8,128]{3,2,1,0:T(8,128)S(1)} copy-done((f32[1,2,8,128]{3,2,1,0:T(8,128)S(1)}, f32[1,2,8,128]{3,2,1,0:T(8,128)}, u32[]{:S(2)}) %copy-start.2) | copy-done | bytes 8216
  5.1 0.0 copy-start.3
  5.1 0.7 %copy-done.3 = f32[1,2,8,128]{3,2,1,0:T(8,128)S(1)} copy-done((f32[1,2,8,128]{3,2,1,0:T(8,128)S(1)}, f32[1,2,8,128]{3,2,1,0:T(8,128)}, u32[]{:S(2)}) %copy-start.3) | copy-done | bytes 8216
  5.8 48.6 %shard_map.64 = f32[2,8,128]{2,1,0:T(8,128)S(1)} custom-call(f32[1,2,8,4,128,128]{5,4,3,2,1,0:T(8,128)S(1)} %copy-done, s32[1,2,8,4]{3,2,1,0:T(8,128)S(1)} %copy.7.columns, s32[1]{0:T(128)S(6)} %copy.9.steps, f32[8,8,128]{2,1,0:T(8,128)S(1)} %copy-done.1, f32[1,2,8,128]{3,2,1,0:T(8,128)S(1)} %copy-done.2, f32[1,2,8,128]{3,2,1,0:T(8,128)S(1)} %copy-done.3), custom_call_target="tpu_custom_call" | custom-call | tf_op jit(solution)/shard_map/pallas_call | solution.py:370
  54.4 0.6 %copy.10 = f32[2,8,128]{2,1,0:T(8,128)} copy(f32[2,8,128]{2,1,0:T(8,128)S(1)} %shard_map.64) | data formatting | bytes 16384
Async XLA Ops:
  1.4 2.2 %copy-start = (f32[1,2,8,4,128,128]{5,4,3,2,1,0:T(8,128)S(1)}, f32[1,2,8,4,128,128]{5,4,3,2,1,0:T(8,128)}, u32[]{:S(2)}) copy-start(f32[1,2,8,4,128,128]{5,4,3,2,1,0:T(8,128)} %tiles.1) | copy-start | bytes 12582916
  3.6 0.8 %copy-start.1 = (f32[8,8,128]{2,1,0:T(8,128)S(1)}, f32[8,8,128]{2,1,0:T(8,128)}, u32[]{:S(2)}) copy-start(f32[8,8,128]{2,1,0:T(8,128)} %direction.1) | copy-start | bytes 98308
  4.4 0.7 %copy-start.2 = (f32[1,2,8,128]{3,2,1,0:T(8,128)S(1)}, f32[1,2,8,128]{3,2,1,0:T(8,128)}, u32[]{:S(2)}) copy-start(f32[1,2,8,128]{3,2,1,0:T(8,128)} %forcing.1) | copy-start | bytes 24580
  5.1 0.7 %copy-start.3 = (f32[1,2,8,128]{3,2,1,0:T(8,128)S(1)}, f32[1,2,8,128]{3,2,1,0:T(8,128)}, u32[]{:S(2)}) copy-start(f32[1,2,8,128]{3,2,1,0:T(8,128)} %observe.1) | copy-start | bytes 24580

commit v2 on v1

--- a/solution.py
+++ b/solution.py
@@ -24,10 +24,13 @@
     tiles,
     columns,
     steps,
+    direction_far,
+    forcing_far,
+    observe_far,
+    out,
     direction,
     forcing,
     observe,
-    out,
     raw,
     weights,
     ext0,
@@ -44,6 +47,7 @@
     brim_out0,
     grad_out,
     grad_in,
+    small_sem,
     load_sem,
     fwd_send,
     fwd_recv,
@@ -57,7 +61,7 @@
     g_recv,
 ):
     dirs, nb, tile = direction.shape
-    slots = columns.shape[3]
+    slots = columns.shape[2]
     width = nb + 2 * HALO
     dpw = dirs // windows
     w = lax.axis_index("tm")
@@ -65,11 +69,21 @@
     has_prev, has_next = w > 0, w < windows - 1
     has_lo, has_hi = p > 0, p < parts - 1
 
-    loads = [
-        pltpu.make_async_copy(tiles.at[0, k], raw.at[k], load_sem.at[k]) for k in range(2)
+    def load(k, b):
+        return pltpu.make_async_copy(tiles.at[0, k, b], raw.at[k, b], load_sem.at[k, b])
+
+    for b in range(nb):
+        load(0, b).start()
+    small = [
+        pltpu.make_async_copy(src, dst, small_sem.at[i])
+        for i, (src, dst) in enumerate(
+            ((direction_far, direction), (forcing_far, forcing), (observe_far, observe))
+        )
     ]
-    for load in loads:
-        load.start()
+    for copy in small:
+        copy.start()
+    for b in range(nb):
+        load(1, b).start()
     for ref in (fin, fhalo, bin_core, bin_rim, bhalo):
         ref[...] = jnp.zeros(ref.shape, F32)
 
@@ -97,7 +111,7 @@
     first = p * nb - HALO
     local = [
         [
-            [jnp.clip(columns[0, k, b, j] - first, 0, width - 1) for j in range(slots)]
+            [jnp.clip(columns[0, k, j, b] - first, 0, width - 1) for j in range(slots)]
             for b in range(nb)
         ]
         for k in range(2)
@@ -106,6 +120,7 @@
 
     def convert(k):
         def row(b, carry):
+            load(k, b).wait()
             for j in range(slots):
                 x = raw[k, b, j]
                 high = x.astype(BF16)
@@ -153,11 +168,15 @@
     order = [*range(HALO), *range(nb - HALO, nb), *range(HALO, nb - HALO)]
     low, high_at = slice(0, HALO), slice(HALO, 2 * HALO)
 
+    convert(0)
+
+    @pl.when(has_prev)
+    def _():
+        convert(1)
+
+    for copy in small:
+        copy.wait()
     load_rows = [direction[:, b, :] for b in range(nb)]
-    loads[0].wait()
-    convert(0)
-    loads[1].wait()
-    convert(1)
 
     def product(k, ext, b):
         lhs = jnp.concatenate([ext[local[k][b][j]] for j in range(slots)], axis=1)
@@ -198,6 +217,11 @@
                 fh_recv.at[1],
                 {"tm": w, "map": p + 1},
             )
+
+    @pl.when(w == 0)
+    def _():
+        convert(1)
+
     arrived(has_hi, fhalo.at[high_at], fh_send.at[0], fh_recv.at[0])
     arrived(has_lo, fhalo.at[low], fh_send.at[1], fh_recv.at[1])
     for q in range(HALO):
@@ -364,15 +388,19 @@
     width = nb + 2 * HALO
     dpw = dirs // windows
     vmem = pl.BlockSpec(memory_space=pltpu.VMEM)
+    hbm = pl.BlockSpec(memory_space=pltpu.HBM)
     smem = pl.BlockSpec(memory_space=pltpu.SMEM)
     block = lambda *lead: pltpu.VMEM((*lead, dirs, tile), F32)
     sems = lambda n: pltpu.SemaphoreType.DMA((n,))
     return pl.pallas_call(
         functools.partial(kernel, windows, parts),
         out_shape=jax.ShapeDtypeStruct((dpw, nb, tile), F32),
-        in_specs=[pl.BlockSpec(memory_space=pl.ANY), smem, smem, vmem, vmem, vmem],
+        in_specs=[hbm, smem, smem, hbm, hbm, hbm],
         out_specs=vmem,
         scratch_shapes=[
+            pltpu.VMEM(direction.shape, F32),
+            pltpu.VMEM(forcing.shape, F32),
+            pltpu.VMEM(observe.shape, F32),
             pltpu.VMEM((2, nb, slots, tile, tile), F32),
             pltpu.VMEM((2, nb, 2 * tile, slots * tile), BF16),
             pltpu.VMEM((width, 2 * dirs, tile), BF16),
@@ -389,7 +417,8 @@
             block(2 * HALO),
             pltpu.VMEM((dirs, nb, tile), F32),
             pltpu.VMEM((windows - 1, dpw, nb, tile), F32),
-            sems(2),
+            sems(3),
+            pltpu.SemaphoreType.DMA((2, nb)),
             sems(5),
             sems(5),
             sems(2),
@@ -402,9 +431,9 @@
             sems(windows - 1),
         ],
         compiler_params=pltpu.CompilerParams(
-            collective_id=0, has_side_effects=True, vmem_limit_bytes=32 * 1024 * 1024
+            collective_id=0, has_side_effects=True, vmem_limit_bytes=63 * 1024 * 1024
         ),
-    )(tiles, columns, window_steps, direction, forcing, observe)
+    )(tiles, jnp.swapaxes(columns, 2, 3), window_steps, direction, forcing, observe)
 
 
 def solution(mesh):

time: 55.3 us -> 51.4 us (0.929)
  local copies, waits for them, and re-layouts: 5.71 us -> 1.3 us
  Pallas kernels: 48.6 us -> 49.2 us
    unnamed x10 -> x1, local copies, waits for them, and re-layouts: 5.71 us -> 1.3 us
    pallas_call x1, Pallas kernels: 48.6 us -> 49.2 us  [shards(): pl.pallas_call(functools.partial(kernel, windows, parts), out_shape=jax.S...]
where the time goes in v2:
time: 51.4 us; the launch traced here: 51.1 us
  Pallas kernels  49.2 us (96%)
  local copies, waits for them, and re-layouts  1.3 us (3%)
  between operations  0.66 us (1%)
    pallas_call x1, Pallas kernels, shards(): pl.pallas_call(functools.partial(kernel, windows, parts), out_shape=jax.S...  49.2 us
    unnamed x1, local copies, waits for them, and re-layouts  1.3 us

profile of v2, /device:TPU:1, one launch (start us, length us, event | category | flops | bytes accessed | tf_op | source)
XLA Modules:
  0.0 51.1 jit_solution(6878879616159970960)
XLA Ops:
  0.7 49.2 %shard_map.64 = f32[2,8,128]{2,1,0:T(8,128)} custom-call(f32[1,2,8,4,128,128]{5,4,3,2,1,0:T(8,128)} %tiles.1, s32[1,2,4,8]{3,2,1,0:T(4,128)} %bitcast.1, s32[1]{0:T(128)S(6)} %copy.8.steps, f32[8,8,128]{2,1,0:T(8,128)} %direction_far.1, f32[1,2,8,128]{3,2,1,0:T(8,128)} %forcing_far.1, f32[1,2,8,128]{3,2,1,0:T(8,128)} %observe_far.1), custom_call_target="tpu_custom_call" | custom-call | tf_op jit(solution)/shard_map/pallas_call | solution.py:395
  49.8 1.3 %copy.9 = f32[2,8,128]{2,1,0:T(8,128)} copy(f32[2,8,128]{2,1,0:T(8,128)} %shard_map.64) | data formatting | bytes 16384

commit v3 on v2

--- a/solution.py
+++ b/solution.py
@@ -33,6 +33,8 @@
     observe,
     raw,
     weights,
+    turned,
+    made,
     ext0,
     ext1,
     state1,
@@ -132,6 +134,19 @@
 
         lax.fori_loop(0, nb, row, 0)
 
+    def turn(k):
+        def row(b, carry):
+            for j in range(slots):
+                x = raw[k, b, j].T
+                high = x.astype(BF16)
+                turned[k, b, j * tile : (j + 1) * tile, :tile] = high
+                turned[k, b, j * tile : (j + 1) * tile, tile:] = (
+                    x - high.astype(F32)
+                ).astype(BF16)
+            return carry
+
+        lax.fori_loop(0, nb, row, 0)
+
     pending = []
 
     def send(ok, src, dst, send_sem, recv_sem, target):
@@ -173,18 +188,33 @@
     @pl.when(has_prev)
     def _():
         convert(1)
+        turn(0)
+        turn(1)
 
     for copy in small:
         copy.wait()
     load_rows = [direction[:, b, :] for b in range(nb)]
 
-    def product(k, ext, b):
-        lhs = jnp.concatenate([ext[local[k][b][j]] for j in range(slots)], axis=1)
-        r = lax.dot_general(
-            lhs, weights[k, b], (((1,), (1,)), ((), ())), preferred_element_type=F32
-        )
-        r = r[:dirs] + r[dirs:]
-        return r[:, :tile] + r[:, tile:]
+    def products(k, ext, rows):
+        def form(array, contracted):
+            for b in rows:
+                lhs = jnp.concatenate([ext[local[k][b][j]] for j in range(slots)], axis=1)
+                r = lax.dot_general(
+                    lhs,
+                    array[k, b],
+                    (((1,), (contracted,)), ((), ())),
+                    preferred_element_type=F32,
+                )
+                r = r[:dirs] + r[dirs:]
+                made[k, b] = r[:, :tile] + r[:, tile:]
+
+        @pl.when(w == 0)
+        def _():
+            form(weights, 1)
+
+        @pl.when(has_prev)
+        def _():
+            form(turned, 0)
 
     for i, (start, size) in enumerate(chunks):
         arrived(has_prev, fin.at[pl.ds(HALO + start, size)], fwd_send.at[i], fwd_recv.at[i])
@@ -195,7 +225,11 @@
     for q in range(width):
         ext0[q] = split(fin[q])
     for n, b in enumerate(order):
-        new = product(0, ext0, b) + forcing[0, 0, b : b + 1] * load_rows[b]
+        if n == 0:
+            products(0, ext0, order[: 2 * HALO])
+        if n == 2 * HALO:
+            products(0, ext0, order[2 * HALO :])
+        new = made[0, b] + forcing[0, 0, b : b + 1] * load_rows[b]
         new = jnp.where(active[0], new, fin[HALO + b])
         state1[b] = new
         ext1[HALO + b] = split(new)
@@ -228,7 +262,11 @@
         ext1[q] = split(fhalo[q])
         ext1[HALO + nb + q] = split(fhalo[HALO + q])
     for n, b in enumerate(order):
-        new = product(1, ext1, b) + forcing[0, 1, b : b + 1] * load_rows[b]
+        if n == 0:
+            products(1, ext1, order[: 2 * HALO])
+        if n == 2 * HALO:
+            products(1, ext1, order[2 * HALO :])
+        new = made[1, b] + forcing[0, 1, b : b + 1] * load_rows[b]
         state2[b] = jnp.where(active[1], new, state1[b])
         if n == HALO - 1:
             send(
@@ -403,6 +441,8 @@
             pltpu.VMEM(observe.shape, F32),
             pltpu.VMEM((2, nb, slots, tile, tile), F32),
             pltpu.VMEM((2, nb, 2 * tile, slots * tile), BF16),
+            pltpu.VMEM((2, nb, slots * tile, 2 * tile), BF16),
+            block(2, nb),
             pltpu.VMEM((width, 2 * dirs, tile), BF16),
             pltpu.VMEM((width, 2 * dirs, tile), BF16),
             block(nb),

time: 51.4 us -> 49.8 us (0.969)
  Pallas kernels: 49.2 us -> 47.6 us
    pallas_call x1, Pallas kernels: 49.2 us -> 47.6 us  [shards(): pl.pallas_call(functools.partial(kernel, windows, parts), out_shape=jax.S...]
where the time goes in v3:
time: 49.8 us; the launch traced here: 49.6 us
  Pallas kernels  47.6 us (96%)
  local copies, waits for them, and re-layouts  1.3 us (3%)
  between operations  0.66 us (1%)
    pallas_call x1, Pallas kernels, shards(): pl.pallas_call(functools.partial(kernel, windows, parts), out_shape=jax.S...  47.6 us
    unnamed x1, local copies, waits for them, and re-layouts  1.3 us

profile of v3, /device:TPU:1, one launch (start us, length us, event | category | flops | bytes accessed | tf_op | source)
XLA Modules:
  0.0 49.6 jit_solution(8273827811872710690)
XLA Ops:
  0.7 47.6 %shard_map.64 = f32[2,8,128]{2,1,0:T(8,128)} custom-call(f32[1,2,8,4,128,128]{5,4,3,2,1,0:T(8,128)} %tiles.1, s32[1,2,4,8]{3,2,1,0:T(4,128)} %bitcast.1, s32[1]{0:T(128)S(6)} %copy.8.steps, f32[8,8,128]{2,1,0:T(8,128)} %direction_far.1, f32[1,2,8,128]{3,2,1,0:T(8,128)} %forcing_far.1, f32[1,2,8,128]{3,2,1,0:T(8,128)} %observe_far.1), custom_call_target="tpu_custom_call" | custom-call | tf_op jit(solution)/shard_map/pallas_call | solution.py:433
  48.3 1.3 %copy.9 = f32[2,8,128]{2,1,0:T(8,128)} copy(f32[2,8,128]{2,1,0:T(8,128)} %shard_map.64) | data formatting | bytes 16384

commit v4 on v3

--- a/solution.py
+++ b/solution.py
@@ -347,29 +347,44 @@
         {"tm": w, "map": p + 1},
     )
     inner = spread[HALO : HALO + nb]
-    spread = [zero] * width
-    after1 = list(carried)
-    for n, b in enumerate([*range(HALO, nb - HALO), *range(HALO), *range(nb - HALO, nb)]):
-        if n == nb - 2 * HALO:
-            arrived(has_hi, bhalo.at[high_at], bh_send.at[0], bh_recv.at[0])
-            arrived(has_lo, bhalo.at[low], bh_send.at[1], bh_recv.at[1])
-        value = inner[b]
-        if b < HALO:
-            value = value + bhalo[b]
-        if b >= nb - HALO:
-            value = value + bhalo[HALO + b - (nb - HALO)]
-        value = jnp.where(active[1], value, carried[b])
-        after1[b] = value
-        a = value + observe[0, 0, b : b + 1] * state1[b]
-        gradient[b] = gradient[b] + jnp.where(
-            active[0], forcing[0, 0, b : b + 1] * a, 0.0
-        )
-        scatter(0, b, a, spread)
-    for q in range(HALO):
-        brim_out0[q] = jnp.where(active[0], spread[q], 0.0)
-        brim_out0[HALO + q] = jnp.where(active[0], spread[HALO + nb + q], 0.0)
-    for b in range(nb):
-        bcore_out[b] = jnp.where(active[0], spread[HALO + b], after1[b])
+    def last_step(handed_on):
+        spread = [zero] * width
+        after1 = list(carried)
+        terms = list(gradient)
+        for n, b in enumerate([*range(HALO, nb - HALO), *range(HALO), *range(nb - HALO, nb)]):
+            if n == nb - 2 * HALO:
+                arrived(has_hi, bhalo.at[high_at], bh_send.at[0], bh_recv.at[0])
+                arrived(has_lo, bhalo.at[low], bh_send.at[1], bh_recv.at[1])
+            value = inner[b]
+            if b < HALO:
+                value = value + bhalo[b]
+            if b >= nb - HALO:
+                value = value + bhalo[HALO + b - (nb - HALO)]
+            value = jnp.where(active[1], value, carried[b])
+            after1[b] = value
+            a = value + observe[0, 0, b : b + 1] * state1[b]
+            terms[b] = terms[b] + jnp.where(
+                active[0], forcing[0, 0, b : b + 1] * a, 0.0
+            )
+            if handed_on:
+                scatter(0, b, a, spread)
+        if handed_on:
+            for q in range(HALO):
+                brim_out0[q] = jnp.where(active[0], spread[q], 0.0)
+                brim_out0[HALO + q] = jnp.where(active[0], spread[HALO + nb + q], 0.0)
+            for b in range(nb):
+                bcore_out[b] = jnp.where(active[0], spread[HALO + b], after1[b])
+        for b in range(nb):
+            grad_out[:, b, :] = terms[b]
+
+    @pl.when(w == 0)
+    def _():
+        last_step(False)
+
+    @pl.when(has_prev)
+    def _():
+        last_step(True)
+
     send(
         has_prev & has_lo,
         brim_out0.at[low],
@@ -395,8 +410,6 @@
         {"tm": w - 1, "map": p},
     )
 
-    for b in range(nb):
-        grad_out[:, b, :] = gradient[b]
     always = w >= 0
     for o in range(1, windows):
         target = lax.rem(w + o, windows)

time: 49.8 us -> 49.6 us (level)
  no operation moved by 1% of the time
where the time goes in v4:
time: 49.6 us; the launch traced here: 49.4 us
  Pallas kernels  47.4 us (96%)
  local copies, waits for them, and re-layouts  1.3 us (3%)
  between operations  0.66 us (1%)
    pallas_call x1, Pallas kernels, shards(): pl.pallas_call(functools.partial(kernel, windows, parts), out_shape=jax.S...  47.4 us
    unnamed x1, local copies, waits for them, and re-layouts  1.3 us

profile of v4, /device:TPU:1, one launch (start us, length us, event | category | flops | bytes accessed | tf_op | source)
XLA Modules:
  0.0 49.4 jit_solution(9346200636893795144)
XLA Ops:
  0.7 47.4 %shard_map.64 = f32[2,8,128]{2,1,0:T(8,128)} custom-call(f32[1,2,8,4,128,128]{5,4,3,2,1,0:T(8,128)} %tiles.1, s32[1,2,4,8]{3,2,1,0:T(4,128)} %bitcast.1, s32[1]{0:T(128)S(6)} %copy.8.steps, f32[8,8,128]{2,1,0:T(8,128)} %direction_far.1, f32[1,2,8,128]{3,2,1,0:T(8,128)} %forcing_far.1, f32[1,2,8,128]{3,2,1,0:T(8,128)} %observe_far.1), custom_call_target="tpu_custom_call" | custom-call | tf_op jit(solution)/shard_map/pallas_call | solution.py:446
  48.1 1.3 %copy.9 = f32[2,8,128]{2,1,0:T(8,128)} copy(f32[2,8,128]{2,1,0:T(8,128)} %shard_map.64) | data formatting | bytes 16384

commit v5 on v3

--- a/solution.py
+++ b/solution.py
@@ -297,6 +297,10 @@
                     {"tm": w + 1, "map": p},
                 )
 
+    held = []
+    rim = [*range(HALO), *range(HALO + nb, width)]
+    core = range(HALO, HALO + nb)
+
     def scatter(k, b, a, spread):
         s = split(a)
         r = lax.dot_general(
@@ -306,11 +310,15 @@
             preferred_element_type=F32,
         )
         r = r[:dirs] + r[dirs:]
-        for j in range(slots):
-            at = jnp.full((dirs, tile), local[k][b][j], jnp.int32)
-            part = r[:, j * tile : (j + 1) * tile]
-            for q in range(width):
-                spread[q] = spread[q] + jnp.where(at == q, part, 0.0)
+        held.append((k, b, r))
+
+    def rims_then_inner(spread, wanted):
+        for k, b, r in held:
+            for j in range(slots):
+                at = jnp.full((dirs, tile), local[k][b][j], jnp.int32)
+                part = r[:, j * tile : (j + 1) * tile]
+                for q in wanted:
+                    spread[q] = spread[q] + jnp.where(at == q, part, 0.0)
 
     seen1 = [observe[0, 1, b : b + 1] * state2[b] for b in range(nb)]
     arrived(has_next, bin_core, bwd_send.at[0], bwd_recv.at[0])
@@ -327,6 +335,7 @@
         a = carried[b] + seen1[b]
         gradient[b] = jnp.where(active[1], forcing[0, 1, b : b + 1] * a, 0.0)
         scatter(1, b, a, spread)
+    rims_then_inner(spread, rim)
     for q in range(HALO):
         brim_out[q] = spread[q]
         brim_out[HALO + q] = spread[HALO + nb + q]
@@ -346,6 +355,8 @@
         bh_recv.at[1],
         {"tm": w, "map": p + 1},
     )
+    rims_then_inner(spread, core)
+    held.clear()
     inner = spread[HALO : HALO + nb]
     spread = [zero] * width
     after1 = list(carried)
@@ -365,11 +376,10 @@
             active[0], forcing[0, 0, b : b + 1] * a, 0.0
         )
         scatter(0, b, a, spread)
+    rims_then_inner(spread, rim)
     for q in range(HALO):
         brim_out0[q] = jnp.where(active[0], spread[q], 0.0)
         brim_out0[HALO + q] = jnp.where(active[0], spread[HALO + nb + q], 0.0)
-    for b in range(nb):
-        bcore_out[b] = jnp.where(active[0], spread[HALO + b], after1[b])
     send(
         has_prev & has_lo,
         brim_out0.at[low],
@@ -386,6 +396,9 @@
         bwd_recv.at[1],
         {"tm": w - 1, "map": p + 1},
     )
+    rims_then_inner(spread, core)
+    for b in range(nb):
+        bcore_out[b] = jnp.where(active[0], spread[HALO + b], after1[b])
     send(
         has_prev,
         bcore_out,

time: 49.8 us -> 49.8 us (level)
  no operation moved by 1% of the time
where the time goes in v5:
time: 49.8 us; the launch traced here: 49.6 us
  Pallas kernels  47.6 us (96%)
  local copies, waits for them, and re-layouts  1.3 us (3%)
  between operations  0.66 us (1%)
    pallas_call x1, Pallas kernels, shards(): pl.pallas_call(functools.partial(kernel, windows, parts), out_shape=jax.S...  47.6 us
    unnamed x1, local copies, waits for them, and re-layouts  1.3 us

profile of v5, /device:TPU:1, one launch (start us, length us, event | category | flops | bytes accessed | tf_op | source)
XLA Modules:
  0.0 49.6 jit_solution(12833459874173146812)
XLA Ops:
  0.7 47.6 %shard_map.64 = f32[2,8,128]{2,1,0:T(8,128)} custom-call(f32[1,2,8,4,128,128]{5,4,3,2,1,0:T(8,128)} %tiles.1, s32[1,2,4,8]{3,2,1,0:T(4,128)} %bitcast.1, s32[1]{0:T(128)S(6)} %copy.8.steps, f32[8,8,128]{2,1,0:T(8,128)} %direction_far.1, f32[1,2,8,128]{3,2,1,0:T(8,128)} %forcing_far.1, f32[1,2,8,128]{3,2,1,0:T(8,128)} %observe_far.1), custom_call_target="tpu_custom_call" | custom-call | tf_op jit(solution)/shard_map/pallas_call | solution.py:446
  48.3 1.3 %copy.9 = f32[2,8,128]{2,1,0:T(8,128)} copy(f32[2,8,128]{2,1,0:T(8,128)} %shard_map.64) | data formatting | bytes 16384
